TPU v7x, 128 devices: a whole 4x4x4 slice. The times are simulated.
128 devices in a mesh: space: 8 (over x, y_lo), tm: 16 (over y_hi, z, core).
Axes of the slice: x: 4, y: 4 (y_hi: 2, y_lo: 2; y = y_hi * 2 + y_lo), z: 4, core: 2. Of those that a mesh axis runs over, the one named last changes fastest.
Arguments:
- snapshots: bfloat16 [24576, 4096], P('space', 'tm'), may hold values from -6 to 6
- coefficients: bfloat16 [4096, 64], replicated, may hold values from -0.09375 to 0.09375
Outputs:
- gram: float32 [4096, 4096], P('space', 'tm')
- modes: bfloat16 [24576, 64], P('space')
- amplitudes: float32 [4096, 64], P('tm')
- residual: bfloat16 [24576, 4096], P('space', 'tm')
All inputs are finite; a program needn't handle non-finite values.
Results may differ from a plain program's by a relative error of at most 0.0034.
Values may be sent and summed in bfloat16 or wider, within the bound.
A program may use at most 128 MiB of HBM per device.

v0:
```python
import jax
import jax.numpy as jnp
from jax import lax
from jax.sharding import PartitionSpec as P


def cross_block(piece, local_block):
    return lax.dot_general(
        piece, local_block, (((0,), (0,)), ((), ())), preferred_element_type=jnp.float32
    )


def body(snapshots, coefficients):
    cell_rows, snap_cols = snapshots.shape
    tm_count = lax.axis_size("tm")
    space_count = lax.axis_size("space")
    tm_index = lax.axis_index("tm")
    space_index = lax.axis_index("space")
    total_snaps = snap_cols * tm_count
    total_cells = cell_rows * space_count
    term = cross_block(lax.all_gather(snapshots, "tm", axis=1, tiled=True), snapshots)
    gram = lax.psum_scatter(term, "space", scatter_dimension=0, tiled=True) / total_cells
    row_count = total_snaps // space_count
    coeff_rows = lax.dynamic_slice_in_dim(coefficients, space_index * row_count, row_count, 0)
    coeff_own = lax.dynamic_slice_in_dim(coefficients, tm_index * snap_cols, snap_cols, 0)
    projected = lax.psum(jnp.dot(snapshots, coeff_own, preferred_element_type=jnp.float32), "tm")
    weight_part = lax.dot_general(
        gram,
        coeff_rows.astype(jnp.float32),
        (((0,), (0,)), ((), ())),
        precision=lax.Precision.HIGHEST,
    )
    weighted = lax.psum(weight_part, "space")
    energy = lax.psum(jnp.sum(coeff_own.astype(jnp.float32) * weighted, axis=0), "tm")
    scale = lax.rsqrt(energy)
    modes = (projected * scale[None, :]).astype(jnp.bfloat16)
    root_cells = jnp.sqrt(jnp.float32(total_cells))
    amplitudes = root_cells * weighted * scale[None, :]
    slow_part = jnp.dot(modes.astype(jnp.float32), amplitudes.T, precision=lax.Precision.HIGHEST)
    residual = (snapshots.astype(jnp.float32) - slow_part / root_cells).astype(jnp.bfloat16)
    return (gram, modes, amplitudes, residual)


def solution(mesh):
    placed = (P("space", "tm"), P())
    return jax.shard_map(
        body,
        mesh=mesh,
        in_specs=placed,
        out_specs=(P("space", "tm"), P("space", None), P("tm", None), P("space", "tm")),
        check_vma=False,
    )
```

profile of v0, /device:TPU:68, one launch (start us, length us, event | category | flops | bytes accessed | tf_op | source)
XLA Modules:
  0.0 496.4 jit_solution(12148790078927543331)
XLA Ops:
  7.2 0.0 all-gather.2.cloned.1.call-start
  7.2 0.7 all-gather.2.cloned.1.call-update
  7.9 0.0 reduce-scatter.2.cloned.1.call-start
  7.9 162.8 %all-gather.2.cloned.1.call-done = bf16[3072,4096]{1,0:T(8,128)(2,1)} async-done(((bf16[3072,256]{1,0:T(8,128)(2,1)}), bf16[3072,4096]{1,0:T(8,128)(2,1)}) %all-gather.2.cloned.1.call-update) | async-done | bytes 25165840 | tf_op jit(solution)/shard_map/all_gather | solution.py:21
  170.7 13.6 %fusion.7 = f32[4096,256]{1,0:T(8,128)} fusion(bf16[3072,4096]{1,0:T(8,128)(2,1)} %all-gather.2.cloned.1.call-done, bf16[3072,256]{1,0:T(8,128)(2,1)} %param.2), kind=kOutput, calls=%fused_computation.14 | convolution fusion | flops 6442450944 | bytes 30932992 | tf_op jit(solution)/shard_map/dot_general | solution.py:8
  184.4 0.0 reduce-scatter.2.cloned.1.call-update
  184.4 0.0 all-reduce.5.cloned.1.call-start
  184.5 89.8 %reduce-scatter.2.cloned.1.call-done = f32[512,256]{1,0:T(8,128)} async-done(((f32[4096,256]{1,0:T(8,128)}), f32[512,256]{1,0:T(8,128)}) %reduce-scatter.2.cloned.1.call-update) | async-done | bytes 524304 | tf_op jit(solution)/shard_map/reduce_scatter | solution.py:22
  274.3 1.1 broadcast_multiply_fusion
  275.4 0.0 copy-start.1
  275.4 1.9 fusion.2
  277.3 0.0 all-reduce.5.cloned.1.call-update
  277.3 0.0 all-reduce.3.cloned.1.call-start
  277.3 0.0 copy-done
  277.4 2.2 convolution_bitcast_fusion
  279.6 0.0 all-reduce.3.cloned.1.call-update
  279.6 68.9 %all-reduce.5.cloned.1.call-done = f32[256,64]{0,1:T(8,128)} async-done(((f32[256,64]{0,1:T(8,128)}), f32[256,64]{0,1:T(8,128)}) %all-reduce.5.cloned.1.call-update) | async-done | bytes 65552 | tf_op jit(solution)/shard_map/psum | solution.py:33
  348.5 0.9 multiply_reduce_fusion
  349.4 24.7 %psum.23 = f32[64]{0:T(128)S(1)} all-reduce(f32[64]{0:T(128)S(1)} %multiply_reduce_fusion), channel_id=1, replica_groups=mesh['space'=8,'tm'=16] {'tm'}, use_global_device_ids=true, to_apply=%region_4.0 | all-reduce | flops 64 | bytes 512 | tf_op jit(solution)/shard_map/psum | solution.py:34
  374.1 0.9 broadcast_multiply_fusion.1
  375.0 110.9 %all-reduce.3.cloned.1.call-done = f32[3072,64]{0,1:T(8,128)} async-done(((f32[3072,64]{0,1:T(8,128)}), f32[3072,64]{0,1:T(8,128)}) %all-reduce.3.cloned.1.call-update) | async-done | bytes 786448 | tf_op jit(solution)/shard_map/psum | solution.py:26
  486.0 1.2 multiply_convert_fusion
  487.2 0.0 copy-start.2
  487.2 2.7 fusion.1
  (6 shorter events, 0.0 us)
Async XLA Ops:
  7.2 163.6 %all-gather.2.cloned.1.call-start = ((), (), s32[]{:S(2)}) async-start(), calls=%async_computation.1 | async-start | bytes 26738688 | tf_op jit(solution)/shard_map/all_gather | solution.py:21
  7.9 266.4 %reduce-scatter.2.cloned.1.call-start = ((), (), s32[]{:S(2)}) async-start(), calls=%async_computation.2 | async-start | bytes 4718592 | tf_op jit(solution)/shard_map/reduce_scatter | solution.py:22
  184.4 93.0 %copy-start = (bf16[3072,256]{1,0:T(8,128)(2,1)S(1)}, bf16[3072,256]{1,0:T(8,128)(2,1)}, u32[]{:S(2)}) copy-start(bf16[3072,256]{1,0:T(8,128)(2,1)} %param.2) | copy-start | bytes 4718596
  184.4 164.1 %all-reduce.5.cloned.1.call-start = ((), (), s32[]{:S(2)}) async-start(), calls=%async_computation.4 | async-start | bytes 131072 | tf_op jit(solution)/shard_map/psum | solution.py:33
  275.4 214.5 %copy-start.1 = (f32[512,256]{1,0:T(8,128)}, f32[512,256]{1,0:T(8,128)S(1)}, u32[]{:S(2)}) copy-start(f32[512,256]{1,0:T(8,128)S(1)} %broadcast_multiply_fusion) | copy-start | bytes 1572868
  277.3 208.7 %all-reduce.3.cloned.1.call-start = ((), (), s32[]{:S(2)}) async-start(), calls=%async_computation.3 | async-start | bytes 1572864 | tf_op jit(solution)/shard_map/psum | solution.py:26
  375.0 114.9 %copy-start.3 = (f32[256,64]{0,1:T(8,128)}, f32[256,64]{0,1:T(8,128)S(1)}, u32[]{:S(2)}) copy-start(f32[256,64]{0,1:T(8,128)S(1)} %broadcast_multiply_fusion.1) | copy-start | bytes 196612
  487.2 2.7 copy-start.2
Sparse Core Ops, SparseCore 0:
  10.3 160.4 all-gather.1
  184.5 89.7 reduce-scatter.1
  277.4 71.0 all-reduce.4
  351.5 134.3 all-reduce.2
where the time goes:
time: 505 us; the launch traced here: 496 us
  waiting for transfers between devices  433 us (86%)
  blocking collectives  24.7 us (5%)
  matrix products  20.4 us (4%)
  between operations  13.8 us (3%)
    all_gather x1, waiting for transfers between devices, body(): lax.all_gather(snapshots, 'tm', axis=1, tiled=True)  163 us
    psum x1, waiting for transfers between devices, body(): lax.psum(jnp.dot(snapshots, coeff_own, preferred_element_type=jnp.float32...  111 us
    reduce_scatter x1, waiting for transfers between devices, body(): lax.psum_scatter(term, 'space', scatter_dimension=0, tiled=True)  89.8 us
    psum x1, waiting for transfers between devices, body(): weighted = lax.psum(weight_part, 'space')  68.9 us
    psum x1, blocking collectives, body(): lax.psum(jnp.sum(coeff_own.astype(jnp.float32) * weighted, axis=0), 'tm')  24.7 us
    dot_general x1, matrix products, cross_block(): lax.dot_general(piece, local_block, (((0,), (0,)), ((), ())), preferred_e...  13.6 us
  transfers between devices with their start and end apart: 4, of which 4 were waited for; matrix products, arithmetic and copies ran while one was open for 1% of the time, Pallas kernels for 0%

commit v1 on v0

v1 whole, which is shorter than its diff:
```python
import jax
import jax.numpy as jnp
from jax import lax
from jax.experimental import pallas as pl
from jax.experimental.pallas import tpu as pltpu
from jax.sharding import PartitionSpec as P

MESH = pl.DeviceIdType.MESH
F32, BF16 = jnp.float32, jnp.bfloat16
CHUNKS = 4


def device_at(x, y, z, c):
    x, y, z = x % 4, y % 4, z % 4
    return (x * 2 + y % 2, (y // 2) * 8 + z * 2 + c)


def wait_for(ref, sem):
    pltpu.make_async_copy(ref, ref, sem).wait()


def split(value):
    high = value.astype(BF16)
    return high, (value - high.astype(F32)).astype(BF16)


def kernel(
    snaps, coeffs, gram, modes, amps, resid,
    own, coef, base, north, south, cross, line_x, sum_x, line_y, mirror, direct, flipped, flip_in,
    part, sib_part, pieces, proj, weight, weights,
    local_sem, y_send, y_recv, sib_send, sib_recv, n_send, n_recv, m_send, m_recv, ms_send, ms_recv,
    x_send, x_recv, l_send, l_recv, d_send, d_recv, t_send, t_recv,
    p_send, p_recv, r_send, r_recv, g_send, g_recv, f_send, f_recv, w_send, w_recv,
):
    space, tm = lax.axis_index("space"), lax.axis_index("tm")
    x, yl, yh, z, c = space // 2, space % 2, tm // 8, (tm // 2) % 4, tm % 2
    y, chip, oh, oc = 2 * yh + yl, tm // 2, 1 - yh, 1 - c
    cells, cols = own.shape
    half, quarter, step = cells // 2, cells // 4, cells // 2 // CHUNKS
    total_cells = cells * 8
    rank = coef.shape[0]
    row_at = 2 * (x % 2) + yl
    role = (row_at - z + 4) % 4
    zs = (z, z, (z + 3) % 4)
    pending = []

    def copy(src, dst, send, recv, device, when=None):
        remote = pltpu.make_async_remote_copy(
            src_ref=src, dst_ref=dst, send_sem=send, recv_sem=recv, device_id=device, device_id_type=MESH
        )
        if when is None:
            remote.start()
        else:
            pl.when(when)(remote.start)
        pending.append((remote, when))

    sibling = device_at(x, y, z, oc)
    partner = device_at(x, y + 2, z, c)
    below, above = device_at(x, y, z + 3, c), device_at(x, y, z + 1, c)

    def turned(at_x, at_y, at_z):
        return 2 * (at_y // 2) + (at_z % 4) // 2, 2 * (at_x // 2) + at_z % 2

    barrier = pltpu.get_barrier_semaphore()

    def greet(device, when=None):
        def do():
            pl.semaphore_signal(barrier, inc=1, device_id=device, device_id_type=MESH)

        do() if when is None else pl.when(when)(do)

    sends = (role == 0) | (role == 3)
    greet(sibling)
    greet(device_at(x, 2 * oh + 1 - yl, z, c))
    for k in range(1, 8):
        greet((space, ((chip + k) % 8) * 2 + c))
        greet(((space + k) % 8, tm))
    from_x, from_y = turned(x, y, z)
    from_z = jnp.where(role == 1, z, z + 1)
    for k in range(2):
        greet(device_at(from_x, from_y, from_z, k), (role == 1) | (role == 2))
    pl.semaphore_wait(barrier, jnp.where(sends, 18, 16))

    keep = pl.ds(pl.multiple_of(yh * half, half), half)
    mine = pltpu.make_async_copy(snaps.at[keep], base.at[yh, c], local_sem.at[0])
    mine.start()
    whole = pltpu.make_async_copy(snaps, own, local_sem.at[1])
    whole.start()
    coef_own = pltpu.make_async_copy(
        coeffs.at[:, pl.ds(pl.multiple_of(tm * cols, cols), cols)], coef, local_sem.at[2]
    )
    coef_own.start()

    for k in range(CHUNKS):
        rows = pl.ds(pl.multiple_of(oh * half + k * step, step), step)
        copy(snaps.at[rows], base.at[yh, c, pl.ds(k * step, step)], y_send.at[k], y_recv.at[k], partner)
    copy(snaps.at[keep], base.at[yh, c], sib_send.at[0], sib_recv.at[0], sibling)
    copy(snaps.at[keep], north.at[yh], n_send.at[0], n_recv.at[0], below)
    piece_for = ((z + 1) % 4) // 2
    rows = pl.ds(pl.multiple_of(yh * half + piece_for * quarter, quarter), quarter)
    copy(snaps.at[rows], south.at[yh, c], m_send.at[0], m_recv.at[0], above)

    coef_own.wait()
    whole.wait()

    @pl.loop(0, 4)
    def _(k):
        at = pl.ds(pl.multiple_of(k * (cells // 4), cells // 4), cells // 4)
        part[:, at] = lax.dot_general(
            coef[...], own[at, :], (((1,), (1,)), ((), ())), preferred_element_type=F32
        )

    other_half = pl.ds(pl.multiple_of(oc * half, half), half)
    copy(part.at[:, other_half], sib_part, p_send, p_recv, sibling)
    wait_for(sib_part, p_recv)
    own_half = pl.ds(pl.multiple_of(c * half, half), half)
    sib_part[...] += part[:, own_half]
    for k in range(1, 8):
        to = (chip + k) % 8
        rows = pl.ds(pl.multiple_of(to * 8, 8), 8)
        copy(sib_part.at[rows], pieces.at[k - 1], r_send.at[k - 1], r_recv.at[k - 1], (space, to * 2 + c))

    def relay(k):
        rows = pl.ds(k * step, step)
        wait_for(base.at[oh, c, rows], y_recv.at[k])
        src = base.at[oh, c, rows]
        copy(src, base.at[oh, c, rows], sib_send.at[1 + k], sib_recv.at[1 + k], sibling)
        copy(src, north.at[oh, rows], n_send.at[1 + k], n_recv.at[1 + k], below)
        inside = pl.ds((k % 2) * step, step)
        copy(
            src, south.at[oh, c, inside], m_send.at[1 + k % 2], m_recv.at[1 + k % 2], above, piece_for == k // 2
        )

    relay(0)

    for k in range(7):
        wait_for(pieces.at[k], r_recv.at[k])
    rows8 = pl.ds(pl.multiple_of(chip * 8, 8), 8)
    piece = sib_part[rows8, :]
    for k in range(7):
        piece = piece + pieces[k]
    proj[c, rows8, :] = piece
    for k in range(1, 8):
        to = (chip + k) % 8
        copy(proj.at[c, rows8], proj.at[c, rows8], g_send.at[k - 1], g_recv.at[k - 1], (space, to * 2 + c))

    relay(1)

    for k in range(1, 8):
        rows = pl.ds(pl.multiple_of(((chip - k + 8) % 8) * 8, 8), 8)
        wait_for(proj.at[c, rows], g_recv.at[k - 1])
    copy(proj.at[c], proj.at[c], f_send, f_recv, sibling)
    wait_for(proj.at[oc], f_recv)

    relay(2)

    sums = jnp.zeros((rank, cols), F32)
    squares = jnp.zeros((rank, 1), F32)
    for k in range(2):
        value = proj[k]
        squares = squares + jnp.sum(value * value, axis=1, keepdims=True)
        high, low = split(value)
        block = own[k * half : (k + 1) * half, :]
        sums = sums + jnp.dot(high, block, preferred_element_type=F32)
        sums = sums + jnp.dot(low, block, preferred_element_type=F32)
    weight[:, :cols] = sums
    weight[:, cols:] = jnp.broadcast_to(squares, (rank, 128))
    for k in range(1, 8):
        copy(weight, weights.at[k - 1], w_send.at[k - 1], w_recv.at[k - 1], ((space + k) % 8, tm))

    relay(3)
    mine.wait()

    wait_for(south.at[yh, c], m_recv.at[0])
    copy(south.at[yh, c], south.at[yh, c], ms_send.at[0], ms_recv.at[0], sibling)

    wait_for(base.at[yh, oc], sib_recv.at[0])
    for k in range(CHUNKS):
        wait_for(base.at[oh, oc, pl.ds(k * step, step)], sib_recv.at[1 + k])

    def multiply(kind, left, right, hc):
        @pl.loop(0, 4)
        def _(k):
            hr, cr = k // 2, k % 2
            cross[kind, hc, hr, pl.ds(pl.multiple_of(cr * cols, cols), cols), :] = lax.dot_general(
                left[hr, cr], right[...], (((0,), (0,)), ((), ())), preferred_element_type=F32
            ).astype(BF16)

    def first(kind, early):
        hc = yh if early else oh
        slot = 0 if early else 1
        for hr in range(2):
            to = 2 * hr + zs[kind] // 2
            away = (x - to + 4) % 4
            copy(
                cross.at[kind, hc, hr], line_x.at[kind, slot, away],
                x_send.at[kind, slot, hr], x_recv.at[kind, slot, away],
                device_at(to, y, z, c), to != x,
            )

    def second(kind, early):
        hc = yh if early else oh
        slot = 0 if early else 1

        @pl.when(x % 2 == zs[kind] // 2)
        def _():
            value = cross[kind, hc, x // 2].astype(F32)
            for k in range(1, 4):
                wait_for(line_x.at[kind, slot, k], x_recv.at[kind, slot, k])
                value = value + line_x[kind, slot, k].astype(F32)
            sum_x[kind, slot] = value.astype(BF16)

        to = 2 * hc + zs[kind] % 2
        away = (y - to + 4) % 4
        copy(
            sum_x.at[kind, slot], line_y.at[kind, away], l_send.at[kind, slot], l_recv.at[kind, away],
            device_at(x, to, z, c), (x % 2 == zs[kind] // 2) & (to != y),
        )

    def third(kind):
        value = sum_x[kind, 0].astype(F32)
        for k in range(1, 4):
            wait_for(line_y.at[kind, k], l_recv.at[kind, k])
            value = value + line_y[kind, k].astype(F32)
        return value / total_cells

    multiply(0, base, base.at[yh, c], yh)
    first(0, True)
    multiply(0, base, base.at[oh, c], oh)
    first(0, False)

    wait_for(north.at[yh], n_recv.at[0])
    multiply(1, base, north.at[yh], yh)
    first(1, True)

    for k in range(2):
        inside = pl.ds(k * step, step)
        wait_for(south.at[oh, c, inside], m_recv.at[1 + k])
    copy(south.at[oh, c], south.at[oh, c], ms_send.at[1], ms_recv.at[1], sibling)
    wait_for(south.at[yh, oc], ms_recv.at[0])
    wait_for(south.at[oh, oc], ms_recv.at[1])
    piece_rows = pl.ds(pl.multiple_of((z // 2) * quarter, quarter), quarter)
    multiply(2, south, north.at[yh, piece_rows], yh)
    first(2, True)

    second(0, True)
    second(0, False)

    for k in range(1, 8):
        wait_for(weights.at[k - 1], w_recv.at[k - 1])
    both = weight[...]
    for k in range(7):
        both = both + weights[k]
    scale = lax.rsqrt(both[:, cols : cols + 1] / total_cells)
    root = jnp.sqrt(jnp.float32(total_cells))
    amplitude = (root * (both[:, :cols] / total_cells)) * scale
    amps[...] = amplitude
    for k in range(2):
        modes[:, k * half : (k + 1) * half] = (proj[k] * scale).astype(BF16)
    high, low = split(amplitude)

    @pl.loop(0, 6)
    def _(k):
        at = pl.ds(pl.multiple_of(k * (cells // 6), cells // 6), cells // 6)
        block = modes[:, at]
        slow = lax.dot_general(block, high, (((0,), (0,)), ((), ())), preferred_element_type=F32)
        slow = slow + lax.dot_general(block, low, (((0,), (0,)), ((), ())), preferred_element_type=F32)
        resid[at, :] = (own[at, :].astype(F32) - slow / root).astype(BF16)

    second(1, True)
    second(2, True)

    for k in range(CHUNKS):
        wait_for(north.at[oh, pl.ds(k * step, step)], n_recv.at[1 + k])
    multiply(1, base, north.at[oh], oh)
    first(1, False)
    multiply(2, south, north.at[oh, piece_rows], oh)
    first(2, False)

    @pl.when(role == 0)
    def _():
        gram[...] = third(0)

    second(1, False)
    second(2, False)

    @pl.when(role == 0)
    def _():
        value = third(1)
        mirror[...] = value.astype(BF16)
        flipped[...] = value.T.astype(BF16)

    @pl.when(role == 3)
    def _():
        value = third(2)
        mirror[...] = value.astype(BF16)
        flipped[...] = value.T.astype(BF16)

    copy(mirror, direct, d_send, d_recv, above, sends)
    to_x, to_y = turned(x, y, z + 1)
    to_z = jnp.where(role == 0, z, z + 3)
    for k in range(2):
        copy(
            flipped.at[:, pl.ds(k * cols, cols)], flip_in.at[c], t_send.at[k], t_recv.at[c],
            device_at(to_x, to_y, to_z, k), sends,
        )

    @pl.when((role == 2) | (role == 3))
    def _():
        wait_for(direct, d_recv)
        gram[...] = direct[...].astype(F32)

    @pl.when((role == 1) | (role == 2))
    def _():
        for k in range(2):
            wait_for(flip_in.at[k], t_recv.at[k])

    @pl.when(role == 1)
    def _():
        for k in range(2):
            gram[k * cols : (k + 1) * cols, :] = flip_in[k].astype(F32)

    @pl.when(role == 2)
    def _():
        for k in range(2):
            gram[k * cols : (k + 1) * cols, :] += flip_in[k].astype(F32)

    for remote, when in pending:
        if when is None:
            remote.wait_send()
        else:
            pl.when(when)(remote.wait_send)


def body(snapshots, coefficients):
    cells, cols = snapshots.shape
    snaps, rank = coefficients.shape
    half, quarter = cells // 2, cells // 4
    dma = pltpu.SemaphoreType.DMA
    rows = 2 * cols
    gram, modes, amps, resid = pl.pallas_call(
        kernel,
        out_shape=(
            jax.ShapeDtypeStruct((rows, cols), F32),
            jax.ShapeDtypeStruct((rank, cells), BF16),
            jax.ShapeDtypeStruct((rank, cols), F32),
            jax.ShapeDtypeStruct((cells, cols), BF16),
        ),
        in_specs=[pl.BlockSpec(memory_space=pl.ANY)] * 2,
        out_specs=[pl.BlockSpec(memory_space=pltpu.VMEM)] * 4,
        scratch_shapes=[
            pltpu.VMEM((cells, cols), BF16),
            pltpu.VMEM((rank, cols), BF16),
            pltpu.VMEM((2, 2, half, cols), BF16),
            pltpu.VMEM((2, half, cols), BF16),
            pltpu.VMEM((2, 2, quarter, cols), BF16),
            pltpu.VMEM((3, 2, 2, rows, cols), BF16),
            pltpu.VMEM((3, 2, 4, rows, cols), BF16),
            pltpu.VMEM((3, 2, rows, cols), BF16),
            pltpu.VMEM((3, 4, rows, cols), BF16),
            pltpu.VMEM((rows, cols), BF16),
            pltpu.VMEM((rows, cols), BF16),
            pltpu.VMEM((cols, rows), BF16),
            pltpu.VMEM((2, cols, cols), BF16),
            pltpu.VMEM((rank, cells), F32),
            pltpu.VMEM((rank, half), F32),
            pltpu.VMEM((7, 8, half), F32),
            pltpu.VMEM((2, rank, half), F32),
            pltpu.VMEM((rank, cols + 128), F32),
            pltpu.VMEM((7, rank, cols + 128), F32),
            dma((3,)),
            dma((CHUNKS,)), dma((CHUNKS,)),
            dma((1 + CHUNKS,)), dma((1 + CHUNKS,)),
            dma((1 + CHUNKS,)), dma((1 + CHUNKS,)),
            dma((3,)), dma((3,)),
            dma((2,)), dma((2,)),
            dma((3, 2, 2)), dma((3, 2, 4)),
            dma((3, 2)), dma((3, 4)),
            dma, dma,
            dma((2,)), dma((2,)),
            dma, dma,
            dma((7,)), dma((7,)),
            dma((7,)), dma((7,)),
            dma, dma,
            dma((7,)), dma((7,)),
        ],
        compiler_params=pltpu.CompilerParams(
            collective_id=0, has_side_effects=True, vmem_limit_bytes=56 << 20
        ),
    )(snapshots, coefficients.T)
    return gram, modes.T, amps.T, resid


def solution(mesh):
    return jax.shard_map(
        body,
        mesh=mesh,
        in_specs=(P("space", "tm"), P()),
        out_specs=(P("space", "tm"), P("space", None), P("tm", None), P("space", "tm")),
        check_vma=False,
    )
```

time: 505 us -> 152 us (0.30)
  the two profiles are of different devices: /device:TPU:68 before, /device:TPU:7 now
where the time goes in v1:
time: 152 us; the launch traced here: 151 us
  Pallas kernels  145 us (95%)
  local copies, waits for them, and re-layouts  5.54 us (4%)
    pallas_call x1, Pallas kernels, body(): pl.pallas_call(kernel, out_shape=(jax.ShapeDtypeStruct((rows, cols), F32)...  145 us
    unnamed x8, local copies, waits for them, and re-layouts  5.54 us

profile of v1, /device:TPU:7, one launch (start us, length us, event | category | flops | bytes accessed | tf_op | source)
XLA Modules:
  0.0 151.4 jit_solution(17320182761563950827)
XLA Ops:
  0.6 145.2 %shard_map.57 = (f32[512,256]{1,0:T(8,128)}, bf16[64,3072]{1,0:T(8,128)(2,1)}, f32[64,256]{1,0:T(8,128)}, bf16[3072,256]{1,0:T(8,128)(2,1)}) custom-call(bf16[3072,256]{1,0:T(8,128)(2,1)} %snaps.1, bf16[64,4096]{1,0:T(8,128)(2,1)} %bitcast.3), custom_call_target="tpu_custom_call" | custom-call | tf_op jit(solution)/shard_map/pallas_call | solution.py:341
  145.8 0.0 copy-start.1
  145.9 0.0 copy-start
  145.9 2.0 %copy.10 = f32[512,256]{1,0:T(8,128)} copy(f32[512,256]{1,0:T(8,128)} %get-tuple-element.16) | data formatting | bytes 1048576
  147.9 1.8 %copy.11 = bf16[3072,64]{0,1:T(8,128)(2,1)} copy(bf16[3072,64]{0,1:T(8,128)(2,1)} %bitcast.4) | data formatting | bytes 786432
  149.6 0.0 copy-done.1
  149.6 0.6 copy.12
  150.3 0.0 copy-done
  150.3 1.1 copy.13
Async XLA Ops:
  145.8 3.8 %copy-start.1 = (f32[64,256]{1,0:T(8,128)S(1)}, f32[64,256]{1,0:T(8,128)}, u32[]{:S(2)}) copy-start(f32[64,256]{1,0:T(8,128)} %get-tuple-element.10) | copy-start | bytes 196612
  145.9 4.4 %copy-start = (bf16[3072,256]{1,0:T(8,128)(2,1)S(1)}, bf16[3072,256]{1,0:T(8,128)(2,1)}, u32[]{:S(2)}) copy-start(bf16[3072,256]{1,0:T(8,128)(2,1)} %get-tuple-element.19) | copy-start | bytes 4718596

commit v2 on v1

v2 whole, which is shorter than its diff:
```python
import jax
import jax.numpy as jnp
from jax import lax
from jax.experimental import pallas as pl
from jax.experimental.pallas import tpu as pltpu
from jax.sharding import PartitionSpec as P

MESH = pl.DeviceIdType.MESH
F32, BF16 = jnp.float32, jnp.bfloat16
CHUNKS = 4


def device_at(x, y, z, c):
    x, y, z = x % 4, y % 4, z % 4
    return (x * 2 + y % 2, (y // 2) * 8 + z * 2 + c)


def wait_for(ref, sem):
    pltpu.make_async_copy(ref, ref, sem).wait()


def split(value):
    high = value.astype(BF16)
    return high, (value - high.astype(F32)).astype(BF16)


def kernel(
    snaps, coeffs, gram, modes, amps, resid,
    own, coef, base, north, south,
    early, early_in, early_sum, early_x, late, late_in, late_sum, late_y,
    diag, diag_in, upright, upright_in, turned, turned_in,
    part, sib_part, pieces, proj, weight, weights,
    local_sem, y_send, y_recv, sib_send, sib_recv, n_send, n_recv, m_send, m_recv, ms_send, ms_recv,
    a_send, a_recv, b_send, b_recv, h_send, h_recv, l_send, l_recv,
    e_send, e_recv, d_send, d_recv, t_send, t_recv,
    p_send, p_recv, r_send, r_recv, g_send, g_recv, f_send, f_recv, w_send, w_recv,
):
    space, tm = lax.axis_index("space"), lax.axis_index("tm")
    x, yl, yh, z, c = space // 2, space % 2, tm // 8, (tm // 2) % 4, tm % 2
    y, chip, oh, ol, oc = 2 * yh + yl, tm // 2, 1 - yh, 1 - yl, 1 - c
    xh, xl = x // 2, x % 2
    cells, cols = own.shape
    half, quarter, step = cells // 2, cells // 4, cells // 2 // CHUNKS
    total_cells = cells * 8
    rank = coef.shape[0]
    role = (2 * xl + yl - z + 4) % 4
    pending = []

    def copy(src, dst, send, recv, device, when=None):
        remote = pltpu.make_async_remote_copy(
            src_ref=src, dst_ref=dst, send_sem=send, recv_sem=recv, device_id=device, device_id_type=MESH
        )
        if when is None:
            remote.start()
        else:
            pl.when(when)(remote.start)
        pending.append((remote, when))

    def place(src, dst, send, recv, device, here):
        copy(src, dst, send, recv, device, jnp.logical_not(here))
        pl.when(here)(pltpu.make_async_copy(src, dst, recv).start)

    sibling = device_at(x, y, z, oc)
    partner = device_at(x, y + 2, z, c)
    beside = device_at(x, 2 * yh + ol, z, c)
    across = device_at(x, 2 * oh + ol, z, c)
    below, above = device_at(x, y, z + 3, c), device_at(x, y, z + 1, c)

    z1, z3 = (z + 1) % 4, (z + 3) % 4
    diag_at = (2 * xh + z // 2, 2 * yh + z % 2)
    diag_here = (xl == z // 2) & (yl == z % 2)
    upright_at = (diag_at, (2 * xh + z3 // 2, 2 * yh + z3 % 2))
    turned_at = (2 * yh + z1 // 2, 2 * xh + z1 % 2)
    turned_here = (turned_at[0] == x) & (turned_at[1] == y) & (xl == c)

    barrier = pltpu.get_barrier_semaphore()

    def greet(device, when=None):
        def do():
            pl.semaphore_signal(barrier, inc=1, device_id=device, device_id_type=MESH)

        do() if when is None else pl.when(when)(do)

    greet(sibling)
    greet(across)
    for k in range(1, 8):
        greet((space, ((chip + k) % 8) * 2 + c))
        greet(((space + k) % 8, tm))
    for i in range(2):
        for j in range(2):
            at_x, at_y = 2 * xh + i, 2 * yh + j
            greet(device_at(at_x, at_y, z, c), (role == 0) & ((xl != i) | (yl != j)))
            greet(device_at(at_x, at_y, z + 3, c), role >= 2)
            from_x, from_y = 2 * yh + c, 2 * xh + j
            here = (from_x == x) & (from_y == y) & (c == i)
            greet(device_at(from_x, from_y, z, i), (role == 1) & jnp.logical_not(here))
            greet(device_at(from_x, from_y, z + 1, i), role == 2)

    keep = pl.ds(pl.multiple_of(yh * half, half), half)
    mine = pltpu.make_async_copy(snaps.at[keep], base.at[yh, c], local_sem.at[0])
    whole = pltpu.make_async_copy(snaps, own, local_sem.at[1])
    coef_own = pltpu.make_async_copy(
        coeffs.at[:, pl.ds(pl.multiple_of(tm * cols, cols), cols)], coef, local_sem.at[2]
    )
    coef_own.start()
    whole.start()
    mine.start()
    coef_own.wait()
    whole.wait()

    @pl.loop(0, 4)
    def _(k):
        at = pl.ds(pl.multiple_of(k * (cells // 4), cells // 4), cells // 4)
        part[:, at] = lax.dot_general(
            coef[...], own[at, :], (((1,), (1,)), ((), ())), preferred_element_type=F32
        )

    pl.semaphore_wait(barrier, 21 - diag_here.astype(jnp.int32) - turned_here.astype(jnp.int32))

    for k in range(CHUNKS):
        rows = pl.ds(pl.multiple_of(oh * half + k * step, step), step)
        copy(snaps.at[rows], base.at[yh, c, pl.ds(k * step, step)], y_send.at[k], y_recv.at[k], partner)
    other_half = pl.ds(pl.multiple_of(oc * half, half), half)
    copy(part.at[:, other_half], sib_part, p_send, p_recv, sibling)
    copy(snaps.at[keep], base.at[yh, c], sib_send.at[0], sib_recv.at[0], sibling)
    copy(snaps.at[keep], north.at[yh], n_send.at[0], n_recv.at[0], below)
    piece_for = z1 // 2
    rows = pl.ds(pl.multiple_of(yh * half + piece_for * quarter, quarter), quarter)
    copy(snaps.at[rows], south.at[yh, c], m_send.at[0], m_recv.at[0], above)

    wait_for(sib_part, p_recv)
    own_half = pl.ds(pl.multiple_of(c * half, half), half)
    sib_part[...] += part[:, own_half]
    for k in range(1, 8):
        to = (chip + k) % 8
        rows = pl.ds(pl.multiple_of(to * 8, 8), 8)
        copy(sib_part.at[rows], pieces.at[k - 1], r_send.at[k - 1], r_recv.at[k - 1], (space, to * 2 + c))

    def relay(k):
        rows = pl.ds(k * step, step)
        wait_for(base.at[oh, c, rows], y_recv.at[k])
        src = base.at[oh, c, rows]
        copy(src, base.at[oh, c, rows], sib_send.at[1 + k], sib_recv.at[1 + k], sibling)
        copy(src, north.at[oh, rows], n_send.at[1 + k], n_recv.at[1 + k], below)
        inside = pl.ds((k % 2) * step, step)
        copy(
            src, south.at[oh, c, inside], m_send.at[1 + k % 2], m_recv.at[1 + k % 2], above, piece_for == k // 2
        )

    relay(0)
    relay(1)

    for k in range(7):
        wait_for(pieces.at[k], r_recv.at[k])
    rows8 = pl.ds(pl.multiple_of(chip * 8, 8), 8)
    piece = sib_part[rows8, :]
    for k in range(7):
        piece = piece + pieces[k]
    proj[c, rows8, :] = piece
    for k in range(1, 8):
        to = (chip + k) % 8
        copy(proj.at[c, rows8], proj.at[c, rows8], g_send.at[k - 1], g_recv.at[k - 1], (space, to * 2 + c))

    relay(2)
    relay(3)
    mine.wait()

    wait_for(south.at[yh, c], m_recv.at[0])
    copy(south.at[yh, c], south.at[yh, c], ms_send.at[0], ms_recv.at[0], sibling)

    wait_for(base.at[yh, oc], sib_recv.at[0])
    for k in range(CHUNKS):
        wait_for(base.at[oh, oc, pl.ds(k * step, step)], sib_recv.at[1 + k])

    def product(left, right, k):
        return lax.dot_general(
            left[k // 2, k % 2], right[...], (((0,), (0,)), ((), ())), preferred_element_type=F32
        ).astype(BF16)

    def early_one(kind, left, right):
        @pl.loop(0, 4)
        def _(k):
            value = product(left, right, k)
            early[kind, 0, k] = value[:, : cols // 2]
            early[kind, 1, k] = value[:, cols // 2 :]

        copy(early.at[kind, ol], early_in.at[kind], a_send.at[kind], a_recv.at[kind], beside)

    def early_two(kind):
        wait_for(early_in.at[kind], a_recv.at[kind])
        early_sum[kind] = (early[kind, yl].astype(F32) + early_in[kind].astype(F32)).astype(BF16)
        for k in range(1, 4):
            copy(
                early_sum.at[kind, (x + k) % 4], early_x.at[kind, k - 1],
                b_send.at[kind, k - 1], b_recv.at[kind, k - 1], device_at(x + k, y, z, c),
            )

    def late_one(kind, left, right):
        @pl.loop(0, 4)
        def _(k):
            late[kind, k] = product(left, right, k)

        for k in range(1, 4):
            copy(
                late.at[kind, (x + k) % 4], late_in.at[kind, k - 1],
                h_send.at[kind, k - 1], h_recv.at[kind, k - 1], device_at(x + k, y, z, c),
            )

    def late_two(kind):
        value = late[kind, x].astype(F32)
        for k in range(3):
            wait_for(late_in.at[kind, k], h_recv.at[kind, k])
            value = value + late_in[kind, k].astype(F32)
        late_sum[kind, 0] = value[:, : cols // 2].astype(BF16)
        late_sum[kind, 1] = value[:, cols // 2 :].astype(BF16)
        copy(late_sum.at[kind, yl], late_y.at[kind, 0], l_send.at[kind, 0], l_recv.at[kind, 0], partner)
        copy(late_sum.at[kind, ol], late_y.at[kind, 1], l_send.at[kind, 1], l_recv.at[kind, 1], across)

    def total(kind):
        value = early_sum[kind, x].astype(F32)
        for k in range(3):
            wait_for(early_x.at[kind, k], b_recv.at[kind, k])
            value = value + early_x[kind, k].astype(F32)
        for k in range(2):
            wait_for(late_y.at[kind, k], l_recv.at[kind, k])
            value = value + late_y[kind, k].astype(F32)
        return value / total_cells

    def deliver(kind):
        value = total(kind)
        k = kind - 1
        upright[k] = value.astype(BF16)
        turned[k] = value.T.astype(BF16)
        at_x, at_y = upright_at[k]
        copy(
            upright.at[k], upright_in.at[xl, yl], d_send.at[k], d_recv.at[2 * xl + yl],
            device_at(at_x, at_y, z + 1, c),
        )
        at_x, at_y = turned_at
        dst, send, recv = turned_in.at[c, yl], t_send.at[k], t_recv.at[2 * c + yl]
        if kind == 1:
            place(turned.at[k], dst, send, recv, device_at(at_x, at_y, z, xl), turned_here)
        else:
            copy(turned.at[k], dst, send, recv, device_at(at_x, at_y, z + 3, xl))

    early_one(0, base, base.at[yh, c])
    late_one(0, base, base.at[oh, c])

    for k in range(2):
        inside = pl.ds(k * step, step)
        wait_for(south.at[oh, c, inside], m_recv.at[1 + k])
    copy(south.at[oh, c], south.at[oh, c], ms_send.at[1], ms_recv.at[1], sibling)

    wait_for(north.at[yh], n_recv.at[0])
    early_one(1, base, north.at[yh])

    for k in range(1, 8):
        rows = pl.ds(pl.multiple_of(((chip - k + 8) % 8) * 8, 8), 8)
        wait_for(proj.at[c, rows], g_recv.at[k - 1])
    copy(proj.at[c], proj.at[c], f_send, f_recv, sibling)

    wait_for(south.at[yh, oc], ms_recv.at[0])
    wait_for(south.at[oh, oc], ms_recv.at[1])
    piece_rows = pl.ds(pl.multiple_of((z // 2) * quarter, quarter), quarter)
    early_one(2, south, north.at[yh, piece_rows])

    early_two(0)

    wait_for(proj.at[oc], f_recv)
    sums = jnp.zeros((rank, cols), F32)
    squares = jnp.zeros((rank, 1), F32)
    for k in range(2):
        value = proj[k]
        squares = squares + jnp.sum(value * value, axis=1, keepdims=True)
        high, low = split(value)
        block = own[k * half : (k + 1) * half, :]
        sums = sums + jnp.dot(high, block, preferred_element_type=F32)
        sums = sums + jnp.dot(low, block, preferred_element_type=F32)
    weight[:, :cols] = sums
    weight[:, cols:] = jnp.broadcast_to(squares, (rank, 128))
    for k in range(1, 8):
        copy(weight, weights.at[k - 1], w_send.at[k - 1], w_recv.at[k - 1], ((space + k) % 8, tm))

    early_two(1)
    early_two(2)
    late_two(0)

    for k in range(CHUNKS):
        wait_for(north.at[oh, pl.ds(k * step, step)], n_recv.at[1 + k])
    late_one(1, base, north.at[oh])
    late_one(2, south, north.at[oh, piece_rows])

    diag[...] = total(0)
    place(
        diag, diag_in.at[xl, yl], e_send, e_recv.at[2 * xl + yl], device_at(*diag_at, z, c), diag_here
    )

    for k in range(1, 8):
        wait_for(weights.at[k - 1], w_recv.at[k - 1])
    both = weight[...]
    for k in range(7):
        both = both + weights[k]
    scale = lax.rsqrt(both[:, cols : cols + 1] / total_cells)
    root = jnp.sqrt(jnp.float32(total_cells))
    amplitude = (root * (both[:, :cols] / total_cells)) * scale
    amps[...] = amplitude
    for k in range(2):
        modes[:, k * half : (k + 1) * half] = (proj[k] * scale).astype(BF16)
    high, low = split(amplitude)

    late_two(1)
    late_two(2)

    @pl.loop(0, 6)
    def _(k):
        at = pl.ds(pl.multiple_of(k * (cells // 6), cells // 6), cells // 6)
        block = modes[:, at]
        slow = lax.dot_general(block, high, (((0,), (0,)), ((), ())), preferred_element_type=F32)
        slow = slow + lax.dot_general(block, low, (((0,), (0,)), ((), ())), preferred_element_type=F32)
        resid[at, :] = (own[at, :].astype(F32) - slow / root).astype(BF16)

    deliver(1)
    deliver(2)

    near = cols // 2

    @pl.when(role == 0)
    def _():
        for i in range(2):
            for j in range(2):
                wait_for(diag_in.at[i, j], e_recv.at[2 * i + j])
                gram[i * cols : (i + 1) * cols, j * near : (j + 1) * near] = diag_in[i, j]

    @pl.when(role >= 2)
    def _():
        for i in range(2):
            for j in range(2):
                wait_for(upright_in.at[i, j], d_recv.at[2 * i + j])
                gram[i * cols : (i + 1) * cols, j * near : (j + 1) * near] = upright_in[i, j].astype(F32)

    @pl.when((role == 1) | (role == 2))
    def _():
        for i in range(2):
            for j in range(2):
                wait_for(turned_in.at[i, j], t_recv.at[2 * i + j])

    @pl.when(role == 1)
    def _():
        for k in range(4):
            gram[k * near : (k + 1) * near, :] = turned_in[k // 2, k % 2].astype(F32)

    @pl.when(role == 2)
    def _():
        for k in range(4):
            gram[k * near : (k + 1) * near, :] += turned_in[k // 2, k % 2].astype(F32)

    for remote, when in pending:
        if when is None:
            remote.wait_send()
        else:
            pl.when(when)(remote.wait_send)


def body(snapshots, coefficients):
    cells, cols = snapshots.shape
    snaps, rank = coefficients.shape
    half, quarter = cells // 2, cells // 4
    dma = pltpu.SemaphoreType.DMA
    rows, near = 2 * cols, cols // 2
    gram, modes, amps, resid = pl.pallas_call(
        kernel,
        out_shape=(
            jax.ShapeDtypeStruct((rows, cols), F32),
            jax.ShapeDtypeStruct((rank, cells), BF16),
            jax.ShapeDtypeStruct((rank, cols), F32),
            jax.ShapeDtypeStruct((cells, cols), BF16),
        ),
        in_specs=[pl.BlockSpec(memory_space=pl.ANY)] * 2,
        out_specs=[pl.BlockSpec(memory_space=pltpu.VMEM)] * 4,
        scratch_shapes=[
            pltpu.VMEM((cells, cols), BF16),
            pltpu.VMEM((rank, cols), BF16),
            pltpu.VMEM((2, 2, half, cols), BF16),
            pltpu.VMEM((2, half, cols), BF16),
            pltpu.VMEM((2, 2, quarter, cols), BF16),
            pltpu.VMEM((3, 2, 4, cols, near), BF16),
            pltpu.VMEM((3, 4, cols, near), BF16),
            pltpu.VMEM((3, 4, cols, near), BF16),
            pltpu.VMEM((3, 3, cols, near), BF16),
            pltpu.VMEM((3, 4, cols, cols), BF16),
            pltpu.VMEM((3, 3, cols, cols), BF16),
            pltpu.VMEM((3, 2, cols, near), BF16),
            pltpu.VMEM((3, 2, cols, near), BF16),
            pltpu.VMEM((cols, near), F32),
            pltpu.VMEM((2, 2, cols, near), F32),
            pltpu.VMEM((2, cols, near), BF16),
            pltpu.VMEM((2, 2, cols, near), BF16),
            pltpu.VMEM((2, near, cols), BF16),
            pltpu.VMEM((2, 2, near, cols), BF16),
            pltpu.VMEM((rank, cells), F32),
            pltpu.VMEM((rank, half), F32),
            pltpu.VMEM((7, 8, half), F32),
            pltpu.VMEM((2, rank, half), F32),
            pltpu.VMEM((rank, cols + 128), F32),
            pltpu.VMEM((7, rank, cols + 128), F32),
            dma((3,)),
            dma((CHUNKS,)), dma((CHUNKS,)),
            dma((1 + CHUNKS,)), dma((1 + CHUNKS,)),
            dma((1 + CHUNKS,)), dma((1 + CHUNKS,)),
            dma((3,)), dma((3,)),
            dma((2,)), dma((2,)),
            dma((3,)), dma((3,)),
            dma((3, 3)), dma((3, 3)),
            dma((3, 3)), dma((3, 3)),
            dma((3, 2)), dma((3, 2)),
            dma, dma((4,)),
            dma((2,)), dma((4,)),
            dma((2,)), dma((4,)),
            dma, dma,
            dma((7,)), dma((7,)),
            dma((7,)), dma((7,)),
            dma, dma,
            dma((7,)), dma((7,)),
        ],
        compiler_params=pltpu.CompilerParams(
            collective_id=0, has_side_effects=True, vmem_limit_bytes=56 << 20
        ),
    )(snapshots, coefficients.T)
    return gram, modes.T, amps.T, resid


def solution(mesh):
    return jax.shard_map(
        body,
        mesh=mesh,
        in_specs=(P("space", "tm"), P()),
        out_specs=(P("space", "tm"), P("space", None), P("tm", None), P("space", "tm")),
        check_vma=False,
    )
```

time: 152 us -> 109 us (0.72)
  the two profiles are of different devices: /device:TPU:7 before, /device:TPU:68 now
where the time goes in v2:
time: 109 us; the launch traced here: 107 us
  Pallas kernels  101 us (93%)
  local copies, waits for them, and re-layouts  5.54 us (5%)
    pallas_call x1, Pallas kernels, body(): pl.pallas_call(kernel, out_shape=(jax.ShapeDtypeStruct((rows, cols), F32)...  101 us
    unnamed x8, local copies, waits for them, and re-layouts  5.54 us

profile of v2, /device:TPU:68, one launch (start us, length us, event | category | flops | bytes accessed | tf_op | source)
XLA Modules:
  0.0 107.2 jit_solution(5152226504115032002)
XLA Ops:
  0.6 101.0 %shard_map.57 = (f32[512,256]{1,0:T(8,128)}, bf16[64,3072]{1,0:T(8,128)(2,1)}, f32[64,256]{1,0:T(8,128)}, bf16[3072,256]{1,0:T(8,128)(2,1)}) custom-call(bf16[3072,256]{1,0:T(8,128)(2,1)} %snaps.1, bf16[64,4096]{1,0:T(8,128)(2,1)} %bitcast.3), custom_call_target="tpu_custom_call" | custom-call | tf_op jit(solution)/shard_map/pallas_call | solution.py:370
  101.6 0.0 copy-start.1
  101.6 0.0 copy-start
  101.6 2.0 %copy.10 = f32[512,256]{1,0:T(8,128)} copy(f32[512,256]{1,0:T(8,128)} %get-tuple-element.16) | data formatting | bytes 1048576
  103.6 1.8 %copy.11 = bf16[3072,64]{0,1:T(8,128)(2,1)} copy(bf16[3072,64]{0,1:T(8,128)(2,1)} %bitcast.4) | data formatting | bytes 786432
  105.4 0.0 copy-done.1
  105.4 0.6 copy.12
  106.0 0.0 copy-done
  106.0 1.1 %copy.13 = bf16[3072,256]{1,0:T(8,128)(2,1)} copy(bf16[3072,256]{1,0:T(8,128)(2,1)S(1)} %copy-done) | data formatting | bytes 3145728
Async XLA Ops:
  101.6 3.8 %copy-start.1 = (f32[64,256]{1,0:T(8,128)S(1)}, f32[64,256]{1,0:T(8,128)}, u32[]{:S(2)}) copy-start(f32[64,256]{1,0:T(8,128)} %get-tuple-element.10) | copy-start | bytes 196612
  101.6 4.4 %copy-start = (bf16[3072,256]{1,0:T(8,128)(2,1)S(1)}, bf16[3072,256]{1,0:T(8,128)(2,1)}, u32[]{:S(2)}) copy-start(bf16[3072,256]{1,0:T(8,128)(2,1)} %get-tuple-element.19) | copy-start | bytes 4718596

commit v3 on v2

v3 whole, which is shorter than its diff:
```python
import jax
import jax.numpy as jnp
from jax import lax
from jax.experimental import pallas as pl
from jax.experimental.pallas import tpu as pltpu
from jax.sharding import PartitionSpec as P

MESH = pl.DeviceIdType.MESH
F32, BF16 = jnp.float32, jnp.bfloat16
CHUNKS = 4


def device_at(x, y, z, c):
    x, y, z = x & 3, y & 3, z & 3
    return (x * 2 + (y & 1), (y >> 1) * 8 + z * 2 + c)


def wait_for(ref, sem):
    pltpu.make_async_copy(ref, ref, sem).wait()


def split(value):
    high = value.astype(BF16)
    return high, (value - high.astype(F32)).astype(BF16)


def kernel(
    snaps, coeffs, gram, modes, amps, resid,
    own, coef, base, north, south,
    early, early_in, early_sum, early_x, late, late_in, late_sum, late_y,
    diag, diag_in, upright, upright_in, turned, turned_in,
    up_late, up_late_in, turned_late, turned_late_in,
    part, sib_part, pieces, proj, weight, weights,
    local_sem, y_send, y_recv, sib_send, sib_recv, n_send, n_recv, m_send, m_recv, ms_send, ms_recv,
    a_send, a_recv, b_send, b_recv, h_send, h_recv, l_send, l_recv,
    e_send, e_recv, d_send, d_recv, t_send, t_recv, q_send, q_recv, v_send, v_recv,
    p_send, p_recv, r_send, r_recv, g_send, g_recv, f_send, f_recv, w_send, w_recv,
):
    space, tm = lax.axis_index("space"), lax.axis_index("tm")
    x, yl, yh, z, c = space >> 1, space & 1, tm >> 3, (tm >> 1) & 3, tm & 1
    y, chip, oh, ol, oc = 2 * yh + yl, tm >> 1, 1 - yh, 1 - yl, 1 - c
    xh, xl = x >> 1, x & 1
    cells, cols = own.shape
    half, quarter, step = cells // 2, cells // 4, cells // 2 // CHUNKS
    total_cells = cells * 8
    rank = coef.shape[0]
    role = (2 * xl + yl - z) & 3
    pending = []

    def copy(src, dst, send, recv, device, when=None):
        remote = pltpu.make_async_remote_copy(
            src_ref=src, dst_ref=dst, send_sem=send, recv_sem=recv, device_id=device, device_id_type=MESH
        )
        if when is None:
            remote.start()
        else:
            pl.when(when)(remote.start)
        pending.append((remote, when))

    def place(src, dst, send, recv, device, here):
        copy(src, dst, send, recv, device, jnp.logical_not(here))
        pl.when(here)(pltpu.make_async_copy(src, dst, recv).start)

    sibling = device_at(x, y, z, oc)
    partner = device_at(x, y + 2, z, c)
    beside = device_at(x, 2 * yh + ol, z, c)
    across = device_at(x, 2 * oh + ol, z, c)
    below, above = device_at(x, y, z + 3, c), device_at(x, y, z + 1, c)

    z1, z3 = (z + 1) & 3, (z + 3) & 3
    diag_at = (2 * xh + (z >> 1), 2 * yh + (z & 1))
    diag_here = (xl == (z >> 1)) & (yl == (z & 1))
    turned_at = (2 * yh + (z1 >> 1), 2 * xh + (z1 & 1))
    turned_here = (turned_at[0] == x) & (turned_at[1] == y) & (xl == c)

    barrier = pltpu.get_barrier_semaphore()

    def greet(device, when=None):
        def do():
            pl.semaphore_signal(barrier, inc=1, device_id=device, device_id_type=MESH)

        do() if when is None else pl.when(when)(do)

    greet(sibling)
    greet(across)
    for k in range(1, 8):
        greet((space, ((chip + k) & 7) * 2 + c))
        greet(((space + k) & 7, tm))

    keep = pl.ds(pl.multiple_of(yh * half, half), half)
    mine = pltpu.make_async_copy(snaps.at[keep], base.at[yh, c], local_sem.at[0])
    whole = pltpu.make_async_copy(snaps, own, local_sem.at[1])
    coef_own = pltpu.make_async_copy(
        coeffs.at[:, pl.ds(pl.multiple_of(tm * cols, cols), cols)], coef, local_sem.at[2]
    )
    coef_own.start()
    whole.start()
    mine.start()
    pl.semaphore_wait(barrier, 16)

    for k in range(CHUNKS):
        rows = pl.ds(pl.multiple_of(oh * half + k * step, step), step)
        copy(snaps.at[rows], base.at[yh, c, pl.ds(k * step, step)], y_send.at[k], y_recv.at[k], partner)
    copy(snaps.at[keep], base.at[yh, c], sib_send.at[0], sib_recv.at[0], sibling)
    copy(snaps.at[keep], north.at[yh], n_send.at[0], n_recv.at[0], below)
    piece_for = z1 >> 1
    rows = pl.ds(pl.multiple_of(yh * half + piece_for * quarter, quarter), quarter)
    copy(snaps.at[rows], south.at[yh, c], m_send.at[0], m_recv.at[0], above)

    coef_own.wait()
    whole.wait()
    part[...] = lax.dot_general(coef[...], own[...], (((1,), (1,)), ((), ())), preferred_element_type=F32)
    other_half = pl.ds(pl.multiple_of(oc * half, half), half)
    copy(part.at[:, other_half], sib_part, p_send, p_recv, sibling)
    wait_for(sib_part, p_recv)
    own_half = pl.ds(pl.multiple_of(c * half, half), half)
    sib_part[...] += part[:, own_half]
    for k in range(1, 8):
        to = (chip + k) & 7
        rows = pl.ds(pl.multiple_of(to * 8, 8), 8)
        copy(sib_part.at[rows], pieces.at[k - 1], r_send.at[k - 1], r_recv.at[k - 1], (space, to * 2 + c))

    def relay(k):
        rows = pl.ds(k * step, step)
        wait_for(base.at[oh, c, rows], y_recv.at[k])
        src = base.at[oh, c, rows]
        copy(src, base.at[oh, c, rows], sib_send.at[1 + k], sib_recv.at[1 + k], sibling)
        copy(src, north.at[oh, rows], n_send.at[1 + k], n_recv.at[1 + k], below)
        inside = pl.ds((k % 2) * step, step)
        copy(
            src, south.at[oh, c, inside], m_send.at[1 + k % 2], m_recv.at[1 + k % 2], above, piece_for == k // 2
        )

    relay(0)
    relay(1)
    relay(2)
    relay(3)

    for k in range(7):
        wait_for(pieces.at[k], r_recv.at[k])
    rows8 = pl.ds(pl.multiple_of(chip * 8, 8), 8)
    piece = sib_part[rows8, :]
    for k in range(7):
        piece = piece + pieces[k]
    proj[c, rows8, :] = piece
    for k in range(1, 8):
        to = (chip + k) & 7
        copy(proj.at[c, rows8], proj.at[c, rows8], g_send.at[k - 1], g_recv.at[k - 1], (space, to * 2 + c))

    mine.wait()

    wait_for(south.at[yh, c], m_recv.at[0])
    copy(south.at[yh, c], south.at[yh, c], ms_send.at[0], ms_recv.at[0], sibling)

    wait_for(base.at[yh, oc], sib_recv.at[0])
    for k in range(CHUNKS):
        wait_for(base.at[oh, oc, pl.ds(k * step, step)], sib_recv.at[1 + k])

    def product(left, right, k):
        return lax.dot_general(
            left[k // 2, k % 2], right[...], (((0,), (0,)), ((), ())), preferred_element_type=F32
        ).astype(BF16)

    def early_one(kind, left, right):
        @pl.loop(0, 4)
        def _(k):
            value = product(left, right, k)
            early[kind, 0, k] = value[:, : cols // 2]
            early[kind, 1, k] = value[:, cols // 2 :]

        copy(early.at[kind, ol], early_in.at[kind], a_send.at[kind], a_recv.at[kind], beside)

    def early_two(kind):
        wait_for(early_in.at[kind], a_recv.at[kind])
        early_sum[kind] = (early[kind, yl].astype(F32) + early_in[kind].astype(F32)).astype(BF16)
        for k in range(1, 4):
            copy(
                early_sum.at[kind, (x + k) & 3], early_x.at[kind, k - 1],
                b_send.at[kind, k - 1], b_recv.at[kind, k - 1], device_at(x + k, y, z, c),
            )

    def late_one(kind, left, right):
        @pl.loop(0, 4)
        def _(k):
            late[kind, k] = product(left, right, k)

        for k in range(1, 4):
            copy(
                late.at[kind, (x + k) & 3], late_in.at[kind, k - 1],
                h_send.at[kind, k - 1], h_recv.at[kind, k - 1], device_at(x + k, y, z, c),
            )

    def late_total(kind):
        value = late[kind, x].astype(F32)
        for k in range(3):
            wait_for(late_in.at[kind, k], h_recv.at[kind, k])
            value = value + late_in[kind, k].astype(F32)
        return value

    def early_total(kind):
        value = early_sum[kind, x].astype(F32)
        for k in range(3):
            wait_for(early_x.at[kind, k], b_recv.at[kind, k])
            value = value + early_x[kind, k].astype(F32)
        return value

    def deliver(kind, value, at_yh, up, up_in, up_send, up_recv, over, over_in, over_send, over_recv):
        k = kind - 1
        up[k] = value.astype(BF16)
        over[k] = value.T.astype(BF16)
        row_at = z if kind == 1 else z3
        copy(
            up.at[k], up_in.at[xl, yl], up_send.at[k], up_recv.at[2 * xl + yl],
            device_at(2 * xh + (row_at >> 1), 2 * at_yh + (row_at & 1), z + 1, c),
        )
        device = device_at(2 * at_yh + (z1 >> 1), 2 * xh + (z1 & 1), z if kind == 1 else z3, xl)
        dst, recv = over_in.at[c, yl], over_recv.at[2 * c + yl]
        if kind == 1 and at_yh is yh:
            place(over.at[k], dst, over_send.at[k], recv, device, turned_here)
        else:
            copy(over.at[k], dst, over_send.at[k], recv, device)

    def deliver_early(kind):
        value = early_total(kind) / total_cells
        deliver(
            kind, value, yh, upright, upright_in, d_send, d_recv, turned, turned_in, t_send, t_recv
        )

    def deliver_late(kind):
        value = late_total(kind) / total_cells
        deliver(
            kind, value, oh, up_late, up_late_in, q_send, q_recv, turned_late, turned_late_in, v_send, v_recv
        )

    early_one(0, base, base.at[yh, c])
    late_one(0, base, base.at[oh, c])

    for k in range(2):
        inside = pl.ds(k * step, step)
        wait_for(south.at[oh, c, inside], m_recv.at[1 + k])
    copy(south.at[oh, c], south.at[oh, c], ms_send.at[1], ms_recv.at[1], sibling)

    wait_for(north.at[yh], n_recv.at[0])
    early_one(1, base, north.at[yh])

    wait_for(south.at[yh, oc], ms_recv.at[0])
    wait_for(south.at[oh, oc], ms_recv.at[1])
    piece_rows = pl.ds(pl.multiple_of((z >> 1) * quarter, quarter), quarter)
    early_one(2, south, north.at[yh, piece_rows])

    early_two(0)

    for k in range(1, 8):
        rows = pl.ds(pl.multiple_of(((chip - k) & 7) * 8, 8), 8)
        wait_for(proj.at[c, rows], g_recv.at[k - 1])
    copy(proj.at[c], proj.at[c], f_send, f_recv, sibling)

    early_two(1)
    early_two(2)

    value = late_total(0)
    late_sum[0] = value[:, : cols // 2].astype(BF16)
    late_sum[1] = value[:, cols // 2 :].astype(BF16)
    copy(late_sum.at[yl], late_y.at[0], l_send.at[0], l_recv.at[0], partner)
    copy(late_sum.at[ol], late_y.at[1], l_send.at[1], l_recv.at[1], across)

    wait_for(proj.at[oc], f_recv)
    sums = jnp.zeros((2 * rank, cols), F32)
    squares = jnp.zeros((rank, 1), F32)
    for k in range(2):
        value = proj[k]
        squares = squares + jnp.sum(value * value, axis=1, keepdims=True)
        sums = sums + jnp.dot(
            jnp.concatenate(split(value), axis=0), own[k * half : (k + 1) * half, :], preferred_element_type=F32
        )
    weight[:, :cols] = sums[:rank] + sums[rank:]
    weight[:, cols:] = jnp.broadcast_to(squares, (rank, 128))
    for k in range(1, 8):
        copy(weight, weights.at[k - 1], w_send.at[k - 1], w_recv.at[k - 1], ((space + k) & 7, tm))

    for k in range(CHUNKS):
        wait_for(north.at[oh, pl.ds(k * step, step)], n_recv.at[1 + k])
    late_one(1, base, north.at[oh])
    late_one(2, south, north.at[oh, piece_rows])

    for k in range(1, 8):
        wait_for(weights.at[k - 1], w_recv.at[k - 1])

    value = early_total(0)
    for k in range(2):
        wait_for(late_y.at[k], l_recv.at[k])
        value = value + late_y[k].astype(F32)
    diag[...] = value / total_cells
    place(
        diag, diag_in.at[xl, yl], e_send, e_recv.at[2 * xl + yl], device_at(*diag_at, z, c), diag_here
    )
    deliver_early(1)
    deliver_early(2)

    both = weight[...]
    for k in range(7):
        both = both + weights[k]
    scale = lax.rsqrt(both[:, cols : cols + 1] / total_cells)
    root = jnp.sqrt(jnp.float32(total_cells))
    amplitude = (root * (both[:, :cols] / total_cells)) * scale
    amps[...] = amplitude
    high, low = split(amplitude)

    deliver_late(1)
    deliver_late(2)

    for k in range(2):
        modes[:, k * half : (k + 1) * half] = (proj[k] * scale).astype(BF16)

    @pl.loop(0, 6)
    def _(k):
        at = pl.ds(pl.multiple_of(k * (cells // 6), cells // 6), cells // 6)
        block = modes[:, at]
        slow = lax.dot_general(block, high, (((0,), (0,)), ((), ())), preferred_element_type=F32)
        slow = slow + lax.dot_general(block, low, (((0,), (0,)), ((), ())), preferred_element_type=F32)
        resid[at, :] = (own[at, :].astype(F32) - slow / root).astype(BF16)

    near = cols // 2

    @pl.when(role == 0)
    def _():
        for i in range(2):
            for j in range(2):
                wait_for(diag_in.at[i, j], e_recv.at[2 * i + j])
                gram[i * cols : (i + 1) * cols, j * near : (j + 1) * near] = diag_in[i, j]

    def block_of(first, first_recv, last, last_recv, i, axis):
        for j in range(2):
            wait_for(first.at[i, j], first_recv.at[2 * i + j])
            wait_for(last.at[i, j], last_recv.at[2 * i + j])
        value = last[i, 0].astype(F32) + last[i, 1].astype(F32)
        return value + jnp.concatenate([first[i, 0], first[i, 1]], axis=axis).astype(F32)

    def upright_block(i):
        return block_of(upright_in, d_recv, up_late_in, q_recv, i, 1)

    def turned_block(i):
        return block_of(turned_in, t_recv, turned_late_in, v_recv, i, 0)

    @pl.when(role == 1)
    def _():
        for i in range(2):
            gram[i * cols : (i + 1) * cols, :] = turned_block(i)

    @pl.when(role == 3)
    def _():
        for i in range(2):
            gram[i * cols : (i + 1) * cols, :] = upright_block(i)

    @pl.when(role == 2)
    def _():
        for i in range(2):
            gram[i * cols : (i + 1) * cols, :] = upright_block(i) + turned_block(i)

    for remote, when in pending:
        if when is None:
            remote.wait_send()
        else:
            pl.when(when)(remote.wait_send)


def hand_over(*refs):
    sources, targets, held, sems = refs[:4], refs[4:8], refs[8:12], refs[12]
    inward = [pltpu.make_async_copy(sources[k], held[k], sems.at[0, k]) for k in range(4)]
    outward = [pltpu.make_async_copy(held[k], targets[k], sems.at[1, k]) for k in range(4)]
    for one in inward:
        one.start()
    for first, then in zip(inward, outward):
        first.wait()
        then.start()
    for one in outward:
        one.wait()


def body(snapshots, coefficients):
    cells, cols = snapshots.shape
    snaps, rank = coefficients.shape
    half, quarter = cells // 2, cells // 4
    dma = pltpu.SemaphoreType.DMA
    rows, near = 2 * cols, cols // 2
    results = pl.pallas_call(
        kernel,
        out_shape=(
            jax.ShapeDtypeStruct((rows, cols), F32),
            jax.ShapeDtypeStruct((rank, cells), BF16),
            jax.ShapeDtypeStruct((rank, cols), F32),
            jax.ShapeDtypeStruct((cells, cols), BF16),
        ),
        in_specs=[pl.BlockSpec(memory_space=pl.ANY)] * 2,
        out_specs=[pl.BlockSpec(memory_space=pltpu.VMEM)] * 4,
        scratch_shapes=[
            pltpu.VMEM((cells, cols), BF16),
            pltpu.VMEM((rank, cols), BF16),
            pltpu.VMEM((2, 2, half, cols), BF16),
            pltpu.VMEM((2, half, cols), BF16),
            pltpu.VMEM((2, 2, quarter, cols), BF16),
            pltpu.VMEM((3, 2, 4, cols, near), BF16),
            pltpu.VMEM((3, 4, cols, near), BF16),
            pltpu.VMEM((3, 4, cols, near), BF16),
            pltpu.VMEM((3, 3, cols, near), BF16),
            pltpu.VMEM((3, 4, cols, cols), BF16),
            pltpu.VMEM((3, 3, cols, cols), BF16),
            pltpu.VMEM((2, cols, near), BF16),
            pltpu.VMEM((2, cols, near), BF16),
            pltpu.VMEM((cols, near), F32),
            pltpu.VMEM((2, 2, cols, near), F32),
            pltpu.VMEM((2, cols, near), BF16),
            pltpu.VMEM((2, 2, cols, near), BF16),
            pltpu.VMEM((2, near, cols), BF16),
            pltpu.VMEM((2, 2, near, cols), BF16),
            pltpu.VMEM((2, cols, cols), BF16),
            pltpu.VMEM((2, 2, cols, cols), BF16),
            pltpu.VMEM((2, cols, cols), BF16),
            pltpu.VMEM((2, 2, cols, cols), BF16),
            pltpu.VMEM((rank, cells), F32),
            pltpu.VMEM((rank, half), F32),
            pltpu.VMEM((7, 8, half), F32),
            pltpu.VMEM((2, rank, half), F32),
            pltpu.VMEM((rank, cols + 128), F32),
            pltpu.VMEM((7, rank, cols + 128), F32),
            dma((3,)),
            dma((CHUNKS,)), dma((CHUNKS,)),
            dma((1 + CHUNKS,)), dma((1 + CHUNKS,)),
            dma((1 + CHUNKS,)), dma((1 + CHUNKS,)),
            dma((3,)), dma((3,)),
            dma((2,)), dma((2,)),
            dma((3,)), dma((3,)),
            dma((3, 3)), dma((3, 3)),
            dma((3, 3)), dma((3, 3)),
            dma((2,)), dma((2,)),
            dma, dma((4,)),
            dma((2,)), dma((4,)),
            dma((2,)), dma((4,)),
            dma((2,)), dma((4,)),
            dma((2,)), dma((4,)),
            dma, dma,
            dma((7,)), dma((7,)),
            dma((7,)), dma((7,)),
            dma, dma,
            dma((7,)), dma((7,)),
        ],
        compiler_params=pltpu.CompilerParams(
            collective_id=0, has_side_effects=True, vmem_limit_bytes=56 << 20
        ),
    )(snapshots, coefficients.T)
    gram, modes, amps, resid = pl.pallas_call(
        hand_over,
        out_shape=tuple(jax.ShapeDtypeStruct(r.shape, r.dtype) for r in results),
        in_specs=[pl.BlockSpec(memory_space=pl.ANY)] * 4,
        out_specs=[pl.BlockSpec(memory_space=pl.ANY)] * 4,
        scratch_shapes=[*(pltpu.VMEM(r.shape, r.dtype) for r in results), dma((2, 4))],
    )(*results)
    return gram, modes.T, amps.T, resid


def solution(mesh):
    return jax.shard_map(
        body,
        mesh=mesh,
        in_specs=(P("space", "tm"), P()),
        out_specs=(P("space", "tm"), P("space", None), P("tm", None), P("space", "tm")),
        check_vma=False,
    )
```

time: 109 us -> 102 us (0.936)
  the two profiles are of different devices: /device:TPU:68 before, /device:TPU:3 now
where the time goes in v3:
time: 102 us
  Pallas kernels  102 us (100%)
    pallas_call x1, Pallas kernels, body(): pl.pallas_call(kernel, out_shape=(jax.ShapeDtypeStruct((rows, cols), F32)...  98.6 us
    pallas_call x1, Pallas kernels, body(): pl.pallas_call(hand_over, out_shape=tuple((jax.ShapeDtypeStruct(r.shape,...  2.93 us

profile of v3, /device:TPU:3, one launch (start us, length us, event | category | flops | bytes accessed | tf_op | source)
XLA Modules:
  0.0 102.2 jit_solution(1648041507019655022)
XLA Ops:
  0.6 98.6 %shard_map.57 = (f32[512,256]{1,0:T(8,128)}, bf16[64,3072]{1,0:T(8,128)(2,1)}, f32[64,256]{1,0:T(8,128)}, bf16[3072,256]{1,0:T(8,128)(2,1)}) custom-call(bf16[3072,256]{1,0:T(8,128)(2,1)} %snaps.1, bf16[64,4096]{1,0:T(8,128)(2,1)} %bitcast.3), custom_call_target="tpu_custom_call" | custom-call | tf_op jit(solution)/shard_map/pallas_call | solution.py:386
  99.3 2.9 %shard_map.58 = (f32[512,256]{1,0:T(8,128)}, bf16[64,3072]{1,0:T(8,128)(2,1)}, f32[64,256]{1,0:T(8,128)}, bf16[3072,256]{1,0:T(8,128)(2,1)}) custom-call(f32[512,256]{1,0:T(8,128)} %get-tuple-element.12.refs_0_, bf16[64,3072]{1,0:T(8,128)(2,1)} %get-tuple-element.13.refs_1_, f32[64,256]{1,0:T(8,128)} %get-tuple-element.14.refs_2_, ...), custom_call_target="tpu_custom_call" | custom-call | tf_op jit(solution)/shard_map/pallas_call | solution.py:451

commit v4 on v3

--- a/solution.py
+++ b/solution.py
@@ -28,12 +28,11 @@
     snaps, coeffs, gram, modes, amps, resid,
     own, coef, base, north, south,
     early, early_in, early_sum, early_x, late, late_in, late_sum, late_y,
-    diag, diag_in, upright, upright_in, turned, turned_in,
-    up_late, up_late_in, turned_late, turned_late_in,
-    part, sib_part, pieces, proj, weight, weights,
+    diag, diag_in, upright, upright_in, turned, turned_in, passing,
+    part, sib_part, pieces, proj, weight, weights, weight_sum,
     local_sem, y_send, y_recv, sib_send, sib_recv, n_send, n_recv, m_send, m_recv, ms_send, ms_recv,
     a_send, a_recv, b_send, b_recv, h_send, h_recv, l_send, l_recv,
-    e_send, e_recv, d_send, d_recv, t_send, t_recv, q_send, q_recv, v_send, v_recv,
+    e_send, e_recv, d_send, d_recv, t_send, t_recv, u_send, u_recv,
     p_send, p_recv, r_send, r_recv, g_send, g_recv, f_send, f_recv, w_send, w_recv,
 ):
     space, tm = lax.axis_index("space"), lax.axis_index("tm")
@@ -41,7 +40,7 @@
     y, chip, oh, ol, oc = 2 * yh + yl, tm >> 1, 1 - yh, 1 - yl, 1 - c
     xh, xl = x >> 1, x & 1
     cells, cols = own.shape
-    half, quarter, step = cells // 2, cells // 4, cells // 2 // CHUNKS
+    half, quarter, near = cells // 2, cells // 4, cols // 2
     total_cells = cells * 8
     rank = coef.shape[0]
     role = (2 * xl + yl - z) & 3
@@ -57,9 +56,9 @@
             pl.when(when)(remote.start)
         pending.append((remote, when))
 
-    def place(src, dst, send, recv, device, here):
-        copy(src, dst, send, recv, device, jnp.logical_not(here))
-        pl.when(here)(pltpu.make_async_copy(src, dst, recv).start)
+    def place(src, dst, send, recv, device, here, when=True):
+        copy(src, dst, send, recv, device, jnp.logical_not(here) & when)
+        pl.when(here & when)(pltpu.make_async_copy(src, dst, recv).start)
 
     sibling = device_at(x, y, z, oc)
     partner = device_at(x, y + 2, z, c)
@@ -99,8 +98,12 @@
     pl.semaphore_wait(barrier, 16)
 
     for k in range(CHUNKS):
-        rows = pl.ds(pl.multiple_of(oh * half + k * step, step), step)
-        copy(snaps.at[rows], base.at[yh, c, pl.ds(k * step, step)], y_send.at[k], y_recv.at[k], partner)
+        rows = pl.ds(pl.multiple_of(oh * half + (k & 1) * quarter, quarter), quarter)
+        columns = pl.ds((k >> 1) * near, near)
+        copy(
+            snaps.at[rows, columns], base.at[yh, c, pl.ds((k & 1) * quarter, quarter), columns],
+            y_send.at[k], y_recv.at[k], partner,
+        )
     copy(snaps.at[keep], base.at[yh, c], sib_send.at[0], sib_recv.at[0], sibling)
     copy(snaps.at[keep], north.at[yh], n_send.at[0], n_recv.at[0], below)
     piece_for = z1 >> 1
@@ -120,15 +123,18 @@
         rows = pl.ds(pl.multiple_of(to * 8, 8), 8)
         copy(sib_part.at[rows], pieces.at[k - 1], r_send.at[k - 1], r_recv.at[k - 1], (space, to * 2 + c))
 
+    def tile(k):
+        return pl.ds((k & 1) * quarter, quarter), pl.ds((k >> 1) * near, near)
+
     def relay(k):
-        rows = pl.ds(k * step, step)
-        wait_for(base.at[oh, c, rows], y_recv.at[k])
-        src = base.at[oh, c, rows]
-        copy(src, base.at[oh, c, rows], sib_send.at[1 + k], sib_recv.at[1 + k], sibling)
-        copy(src, north.at[oh, rows], n_send.at[1 + k], n_recv.at[1 + k], below)
-        inside = pl.ds((k % 2) * step, step)
+        rows, columns = tile(k)
+        src = base.at[oh, c, rows, columns]
+        wait_for(src, y_recv.at[k])
+        copy(src, src, sib_send.at[1 + k], sib_recv.at[1 + k], sibling)
+        copy(src, north.at[oh, rows, columns], n_send.at[1 + k], n_recv.at[1 + k], below)
         copy(
-            src, south.at[oh, c, inside], m_send.at[1 + k % 2], m_recv.at[1 + k % 2], above, piece_for == k // 2
+            src, south.at[oh, c, :, columns], m_send.at[1 + (k >> 1)], m_recv.at[1 + (k >> 1)], above,
+            piece_for == (k & 1),
         )
 
     relay(0)
@@ -154,7 +160,7 @@
 
     wait_for(base.at[yh, oc], sib_recv.at[0])
     for k in range(CHUNKS):
-        wait_for(base.at[oh, oc, pl.ds(k * step, step)], sib_recv.at[1 + k])
+        wait_for(base.at[(oh, oc, *tile(k))], sib_recv.at[1 + k])
 
     def product(left, right, k):
         return lax.dot_general(
@@ -179,65 +185,87 @@
                 b_send.at[kind, k - 1], b_recv.at[kind, k - 1], device_at(x + k, y, z, c),
             )
 
-    def late_one(kind, left, right):
+    def send_late(kind, q):
+        for k in range(1, 4):
+            to = (x + k) & 3
+            src, dst = late.at[kind, to], late_in.at[kind, k - 1]
+            if kind:
+                src, dst = src.at[q], dst.at[q]
+            copy(src, dst, h_send.at[kind, k - 1, q], h_recv.at[kind, k - 1, q], device_at(x + k, y, z, c))
+
+    def late_one(kind, left, right, q):
         @pl.loop(0, 4)
         def _(k):
-            late[kind, k] = product(left, right, k)
-
-        for k in range(1, 4):
-            copy(
-                late.at[kind, (x + k) & 3], late_in.at[kind, k - 1],
-                h_send.at[kind, k - 1], h_recv.at[kind, k - 1], device_at(x + k, y, z, c),
-            )
-
-    def late_total(kind):
-        value = late[kind, x].astype(F32)
+            late[kind, k, q] = product(left, right, k)
+
+        send_late(kind, q)
+
+    def late_two(kind, q):
+        value = late[kind, x, q].astype(F32)
         for k in range(3):
-            wait_for(late_in.at[kind, k], h_recv.at[kind, k])
-            value = value + late_in[kind, k].astype(F32)
-        return value
-
-    def early_total(kind):
+            if kind:
+                wait_for(late_in.at[kind, k, q], h_recv.at[kind, k, q])
+            value = value + late_in[kind, k, q].astype(F32)
+        late_sum[kind, q] = value.astype(BF16)
+        copy(
+            late_sum.at[kind, q], late_y.at[kind, yl ^ q], l_send.at[kind, q], l_recv.at[kind, yl ^ q],
+            device_at(x, 2 * oh + q, z, c),
+        )
+
+    def total(kind):
         value = early_sum[kind, x].astype(F32)
         for k in range(3):
             wait_for(early_x.at[kind, k], b_recv.at[kind, k])
             value = value + early_x[kind, k].astype(F32)
-        return value
-
-    def deliver(kind, value, at_yh, up, up_in, up_send, up_recv, over, over_in, over_send, over_recv):
-        k = kind - 1
-        up[k] = value.astype(BF16)
-        over[k] = value.T.astype(BF16)
-        row_at = z if kind == 1 else z3
-        copy(
-            up.at[k], up_in.at[xl, yl], up_send.at[k], up_recv.at[2 * xl + yl],
-            device_at(2 * xh + (row_at >> 1), 2 * at_yh + (row_at & 1), z + 1, c),
-        )
-        device = device_at(2 * at_yh + (z1 >> 1), 2 * xh + (z1 & 1), z if kind == 1 else z3, xl)
-        dst, recv = over_in.at[c, yl], over_recv.at[2 * c + yl]
-        if kind == 1 and at_yh is yh:
-            place(over.at[k], dst, over_send.at[k], recv, device, turned_here)
-        else:
-            copy(over.at[k], dst, over_send.at[k], recv, device)
-
-    def deliver_early(kind):
-        value = early_total(kind) / total_cells
-        deliver(
-            kind, value, yh, upright, upright_in, d_send, d_recv, turned, turned_in, t_send, t_recv
-        )
-
-    def deliver_late(kind):
-        value = late_total(kind) / total_cells
-        deliver(
-            kind, value, oh, up_late, up_late_in, q_send, q_recv, turned_late, turned_late_in, v_send, v_recv
+        for k in range(2):
+            wait_for(late_y.at[kind, k], l_recv.at[kind, k])
+            value = value + late_y[kind, k].astype(F32)
+        return value / total_cells
+
+    def deliver(when):
+        @pl.when(when)
+        def _():
+            for k in range(2):
+                value = total(k + 1)
+                upright[k] = value.astype(BF16)
+                turned[k] = value.T.astype(BF16)
+
+        for k in range(2):
+            dst, send, recv = turned_in.at[c, yl], t_send.at[k], t_recv.at[2 * c + yl]
+            if k == 0:
+                place(turned.at[k], dst, send, recv, device_at(*turned_at, z, xl), turned_here, when)
+            else:
+                copy(turned.at[k], passing, send, u_recv, below, when)
+            row_at = z3 if k else z
+            copy(
+                upright.at[k], upright_in.at[xl, yl], d_send.at[k], d_recv.at[2 * xl + yl],
+                device_at(2 * xh + (row_at >> 1), 2 * yh + (row_at & 1), z + 1, c), when,
+            )
+
+    def pass_on(when):
+        @pl.when(when)
+        def _():
+            wait_for(passing, u_recv)
+
+        two = z ^ 2
+        at_x, at_y = 2 * yh + (two >> 1), 2 * xh + (two & 1)
+        here = (at_x == x) & (at_y == y) & (xl == c)
+        place(
+            passing, turned_in.at[c, yl], u_send, t_recv.at[2 * c + yl], device_at(at_x, at_y, z, xl), here, when
         )
 
     early_one(0, base, base.at[yh, c])
-    late_one(0, base, base.at[oh, c])
+
+    @pl.loop(0, 4)
+    def _(k):
+        value = product(base, base.at[oh, c], k)
+        late[0, k, 0] = value[:, :near]
+        late[0, k, 1] = value[:, near:]
+
+    send_late(0, 0)
 
     for k in range(2):
-        inside = pl.ds(k * step, step)
-        wait_for(south.at[oh, c, inside], m_recv.at[1 + k])
+        wait_for(south.at[oh, c, :, pl.ds(k * near, near)], m_recv.at[1 + k])
     copy(south.at[oh, c], south.at[oh, c], ms_send.at[1], ms_recv.at[1], sibling)
 
     wait_for(north.at[yh], n_recv.at[0])
@@ -258,11 +286,10 @@
     early_two(1)
     early_two(2)
 
-    value = late_total(0)
-    late_sum[0] = value[:, : cols // 2].astype(BF16)
-    late_sum[1] = value[:, cols // 2 :].astype(BF16)
-    copy(late_sum.at[yl], late_y.at[0], l_send.at[0], l_recv.at[0], partner)
-    copy(late_sum.at[ol], late_y.at[1], l_send.at[1], l_recv.at[1], across)
+    for k in range(3):
+        wait_for(late_in.at[0, k], h_recv.at[0, k, 0])
+    late_two(0, 0)
+    late_two(0, 1)
 
     wait_for(proj.at[oc], f_recv)
     sums = jnp.zeros((2 * rank, cols), F32)
@@ -275,42 +302,44 @@
         )
     weight[:, :cols] = sums[:rank] + sums[rank:]
     weight[:, cols:] = jnp.broadcast_to(squares, (rank, 128))
-    for k in range(1, 8):
-        copy(weight, weights.at[k - 1], w_send.at[k - 1], w_recv.at[k - 1], ((space + k) & 7, tm))
-
-    for k in range(CHUNKS):
-        wait_for(north.at[oh, pl.ds(k * step, step)], n_recv.at[1 + k])
-    late_one(1, base, north.at[oh])
-    late_one(2, south, north.at[oh, piece_rows])
-
-    for k in range(1, 8):
-        wait_for(weights.at[k - 1], w_recv.at[k - 1])
-
-    value = early_total(0)
-    for k in range(2):
-        wait_for(late_y.at[k], l_recv.at[k])
-        value = value + late_y[k].astype(F32)
-    diag[...] = value / total_cells
+    for k in range(1, 4):
+        copy(weight, weights.at[k - 1], w_send.at[k - 1], w_recv.at[k - 1], device_at(x + k, y, z, c))
+
+    for q in range(2):
+        columns = pl.ds(q * near, near)
+        for k in range(2):
+            wait_for(north.at[(oh, *tile(2 * q + k))], n_recv.at[1 + 2 * q + k])
+        late_one(1, base, north.at[oh, :, columns], q)
+        late_one(2, south, north.at[oh, piece_rows, columns], q)
+        if q == 0:
+            for k in range(3):
+                wait_for(weights.at[k], w_recv.at[k])
+            weight_sum[...] = (weight[...] + weights[0]) + (weights[1] + weights[2])
+            copy(weight_sum, weights.at[3], w_send.at[3], w_recv.at[3], beside)
+            late_two(1, 0)
+            late_two(2, 0)
+
+    wait_for(weights.at[3], w_recv.at[3])
+    diag[...] = total(0)
     place(
         diag, diag_in.at[xl, yl], e_send, e_recv.at[2 * xl + yl], device_at(*diag_at, z, c), diag_here
     )
-    deliver_early(1)
-    deliver_early(2)
-
-    both = weight[...]
-    for k in range(7):
-        both = both + weights[k]
+
+    deliver(yl == 0)
+    late_two(1, 1)
+    late_two(2, 1)
+    pass_on(yl == 0)
+    both = weight_sum[...] + weights[3]
     scale = lax.rsqrt(both[:, cols : cols + 1] / total_cells)
     root = jnp.sqrt(jnp.float32(total_cells))
     amplitude = (root * (both[:, :cols] / total_cells)) * scale
     amps[...] = amplitude
     high, low = split(amplitude)
 
-    deliver_late(1)
-    deliver_late(2)
-
     for k in range(2):
         modes[:, k * half : (k + 1) * half] = (proj[k] * scale).astype(BF16)
+
+    deliver(yl == 1)
 
     @pl.loop(0, 6)
     def _(k):
@@ -320,7 +349,7 @@
         slow = slow + lax.dot_general(block, low, (((0,), (0,)), ((), ())), preferred_element_type=F32)
         resid[at, :] = (own[at, :].astype(F32) - slow / root).astype(BF16)
 
-    near = cols // 2
+    pass_on(yl == 1)
 
     @pl.when(role == 0)
     def _():
@@ -329,18 +358,16 @@
                 wait_for(diag_in.at[i, j], e_recv.at[2 * i + j])
                 gram[i * cols : (i + 1) * cols, j * near : (j + 1) * near] = diag_in[i, j]
 
-    def block_of(first, first_recv, last, last_recv, i, axis):
+    def block_of(tiles, recv, i, axis):
         for j in range(2):
-            wait_for(first.at[i, j], first_recv.at[2 * i + j])
-            wait_for(last.at[i, j], last_recv.at[2 * i + j])
-        value = last[i, 0].astype(F32) + last[i, 1].astype(F32)
-        return value + jnp.concatenate([first[i, 0], first[i, 1]], axis=axis).astype(F32)
+            wait_for(tiles.at[i, j], recv.at[2 * i + j])
+        return jnp.concatenate([tiles[i, 0], tiles[i, 1]], axis=axis).astype(F32)
 
     def upright_block(i):
-        return block_of(upright_in, d_recv, up_late_in, q_recv, i, 1)
+        return block_of(upright_in, d_recv, i, 1)
 
     def turned_block(i):
-        return block_of(turned_in, t_recv, turned_late_in, v_recv, i, 0)
+        return block_of(turned_in, t_recv, i, 0)
 
     @pl.when(role == 1)
     def _():
@@ -403,26 +430,24 @@
             pltpu.VMEM((3, 4, cols, near), BF16),
             pltpu.VMEM((3, 4, cols, near), BF16),
             pltpu.VMEM((3, 3, cols, near), BF16),
-            pltpu.VMEM((3, 4, cols, cols), BF16),
-            pltpu.VMEM((3, 3, cols, cols), BF16),
-            pltpu.VMEM((2, cols, near), BF16),
-            pltpu.VMEM((2, cols, near), BF16),
+            pltpu.VMEM((3, 4, 2, cols, near), BF16),
+            pltpu.VMEM((3, 3, 2, cols, near), BF16),
+            pltpu.VMEM((3, 2, cols, near), BF16),
+            pltpu.VMEM((3, 2, cols, near), BF16),
             pltpu.VMEM((cols, near), F32),
             pltpu.VMEM((2, 2, cols, near), F32),
             pltpu.VMEM((2, cols, near), BF16),
             pltpu.VMEM((2, 2, cols, near), BF16),
             pltpu.VMEM((2, near, cols), BF16),
             pltpu.VMEM((2, 2, near, cols), BF16),
-            pltpu.VMEM((2, cols, cols), BF16),
-            pltpu.VMEM((2, 2, cols, cols), BF16),
-            pltpu.VMEM((2, cols, cols), BF16),
-            pltpu.VMEM((2, 2, cols, cols), BF16),
+            pltpu.VMEM((near, cols), BF16),
             pltpu.VMEM((rank, cells), F32),
             pltpu.VMEM((rank, half), F32),
             pltpu.VMEM((7, 8, half), F32),
             pltpu.VMEM((2, rank, half), F32),
             pltpu.VMEM((rank, cols + 128), F32),
-            pltpu.VMEM((7, rank, cols + 128), F32),
+            pltpu.VMEM((4, rank, cols + 128), F32),
+            pltpu.VMEM((rank, cols + 128), F32),
             dma((3,)),
             dma((CHUNKS,)), dma((CHUNKS,)),
             dma((1 + CHUNKS,)), dma((1 + CHUNKS,)),
@@ -431,18 +456,17 @@
             dma((2,)), dma((2,)),
             dma((3,)), dma((3,)),
             dma((3, 3)), dma((3, 3)),
-            dma((3, 3)), dma((3, 3)),
-            dma((2,)), dma((2,)),
+            dma((3, 3, 2)), dma((3, 3, 2)),
+            dma((3, 2)), dma((3, 2)),
             dma, dma((4,)),
             dma((2,)), dma((4,)),
             dma((2,)), dma((4,)),
-            dma((2,)), dma((4,)),
-            dma((2,)), dma((4,)),
+            dma, dma,
             dma, dma,
             dma((7,)), dma((7,)),
             dma((7,)), dma((7,)),
             dma, dma,
-            dma((7,)), dma((7,)),
+            dma((4,)), dma((4,)),
         ],
         compiler_params=pltpu.CompilerParams(
             collective_id=0, has_side_effects=True, vmem_limit_bytes=56 << 20

time: 102 us -> 97.1 us (0.952)
  the two profiles are of different devices: /device:TPU:3 before, /device:TPU:68 now
where the time goes in v4:
time: 97.1 us; the launch traced here: 97 us
  Pallas kernels  96.3 us (99%)
    pallas_call x1, Pallas kernels, body(): pl.pallas_call(kernel, out_shape=(jax.ShapeDtypeStruct((rows, cols), F32)...  93.4 us
    pallas_call x1, Pallas kernels, body(): pl.pallas_call(hand_over, out_shape=tuple((jax.ShapeDtypeStruct(r.shape,...  2.93 us

profile of v4, /device:TPU:68, one launch (start us, length us, event | category | flops | bytes accessed | tf_op | source)
XLA Modules:
  0.0 97.0 jit_solution(5631149495265538167)
XLA Ops:
  0.6 93.4 %shard_map.57 = (f32[512,256]{1,0:T(8,128)}, bf16[64,3072]{1,0:T(8,128)(2,1)}, f32[64,256]{1,0:T(8,128)}, bf16[3072,256]{1,0:T(8,128)(2,1)}) custom-call(bf16[3072,256]{1,0:T(8,128)(2,1)} %snaps.1, bf16[64,4096]{1,0:T(8,128)(2,1)} %bitcast.3), custom_call_target="tpu_custom_call" | custom-call | tf_op jit(solution)/shard_map/pallas_call | solution.py:413
  94.1 2.9 %shard_map.58 = (f32[512,256]{1,0:T(8,128)}, bf16[64,3072]{1,0:T(8,128)(2,1)}, f32[64,256]{1,0:T(8,128)}, bf16[3072,256]{1,0:T(8,128)(2,1)}) custom-call(f32[512,256]{1,0:T(8,128)} %get-tuple-element.12.refs_0_, bf16[64,3072]{1,0:T(8,128)(2,1)} %get-tuple-element.13.refs_1_, f32[64,256]{1,0:T(8,128)} %get-tuple-element.14.refs_2_, ...), custom_call_target="tpu_custom_call" | custom-call | tf_op jit(solution)/shard_map/pallas_call | solution.py:475

commit v5 on v4

--- a/solution.py
+++ b/solution.py
@@ -80,11 +80,12 @@
 
         do() if when is None else pl.when(when)(do)
 
-    greet(sibling)
-    greet(across)
+    for device in (sibling, beside):
+        greet(device)
     for k in range(1, 8):
         greet((space, ((chip + k) & 7) * 2 + c))
-        greet(((space + k) & 7, tm))
+    for k in range(1, 4):
+        greet(device_at(x + k, y, z, c))
 
     keep = pl.ds(pl.multiple_of(yh * half, half), half)
     mine = pltpu.make_async_copy(snaps.at[keep], base.at[yh, c], local_sem.at[0])
@@ -95,7 +96,7 @@
     coef_own.start()
     whole.start()
     mine.start()
-    pl.semaphore_wait(barrier, 16)
+    pl.semaphore_wait(barrier, 12)
 
     for k in range(CHUNKS):
         rows = pl.ds(pl.multiple_of(oh * half + (k & 1) * quarter, quarter), quarter)
@@ -278,19 +279,35 @@
 
     early_two(0)
 
+    early_two(1)
+    early_two(2)
+
+    for k in range(3):
+        wait_for(late_in.at[0, k], h_recv.at[0, k, 0])
+    late_two(0, 0)
+    late_two(0, 1)
+
+    for q in range(2):
+        columns = pl.ds(q * near, near)
+        for k in range(2):
+            wait_for(north.at[(oh, *tile(2 * q + k))], n_recv.at[1 + 2 * q + k])
+        late_one(1, base, north.at[oh, :, columns], q)
+        late_one(2, south, north.at[oh, piece_rows, columns], q)
+        if q == 0:
+            late_two(1, 0)
+            late_two(2, 0)
+
     for k in range(1, 8):
         rows = pl.ds(pl.multiple_of(((chip - k) & 7) * 8, 8), 8)
         wait_for(proj.at[c, rows], g_recv.at[k - 1])
     copy(proj.at[c], proj.at[c], f_send, f_recv, sibling)
 
-    early_two(1)
-    early_two(2)
-
-    for k in range(3):
-        wait_for(late_in.at[0, k], h_recv.at[0, k, 0])
-    late_two(0, 0)
-    late_two(0, 1)
-
+    diag[...] = total(0)
+    place(
+        diag, diag_in.at[xl, yl], e_send, e_recv.at[2 * xl + yl], device_at(*diag_at, z, c), diag_here
+    )
+
+    deliver(yl == 0)
     wait_for(proj.at[oc], f_recv)
     sums = jnp.zeros((2 * rank, cols), F32)
     squares = jnp.zeros((rank, 1), F32)
@@ -305,30 +322,15 @@
     for k in range(1, 4):
         copy(weight, weights.at[k - 1], w_send.at[k - 1], w_recv.at[k - 1], device_at(x + k, y, z, c))
 
-    for q in range(2):
-        columns = pl.ds(q * near, near)
-        for k in range(2):
-            wait_for(north.at[(oh, *tile(2 * q + k))], n_recv.at[1 + 2 * q + k])
-        late_one(1, base, north.at[oh, :, columns], q)
-        late_one(2, south, north.at[oh, piece_rows, columns], q)
-        if q == 0:
-            for k in range(3):
-                wait_for(weights.at[k], w_recv.at[k])
-            weight_sum[...] = (weight[...] + weights[0]) + (weights[1] + weights[2])
-            copy(weight_sum, weights.at[3], w_send.at[3], w_recv.at[3], beside)
-            late_two(1, 0)
-            late_two(2, 0)
-
-    wait_for(weights.at[3], w_recv.at[3])
-    diag[...] = total(0)
-    place(
-        diag, diag_in.at[xl, yl], e_send, e_recv.at[2 * xl + yl], device_at(*diag_at, z, c), diag_here
-    )
-
-    deliver(yl == 0)
     late_two(1, 1)
     late_two(2, 1)
+    for k in range(3):
+        wait_for(weights.at[k], w_recv.at[k])
+    weight_sum[...] = (weight[...] + weights[0]) + (weights[1] + weights[2])
+    copy(weight_sum, weights.at[3], w_send.at[3], w_recv.at[3], beside)
     pass_on(yl == 0)
+    deliver(yl == 1)
+    wait_for(weights.at[3], w_recv.at[3])
     both = weight_sum[...] + weights[3]
     scale = lax.rsqrt(both[:, cols : cols + 1] / total_cells)
     root = jnp.sqrt(jnp.float32(total_cells))
@@ -339,7 +341,6 @@
     for k in range(2):
         modes[:, k * half : (k + 1) * half] = (proj[k] * scale).astype(BF16)
 
-    deliver(yl == 1)
 
     @pl.loop(0, 6)
     def _(k):

time: 97.1 us -> 95.2 us (0.980); the launches traced: 97 us -> 93.5 us
  Pallas kernels: 96.3 us -> 92.9 us
    pallas_call x1, Pallas kernels: 93.4 us -> 90 us  [body(): pl.pallas_call(kernel, out_shape=(jax.ShapeDtypeStruct((rows, cols), F32)...]
where the time goes in v5:
time: 95.2 us; the launch traced here: 93.5 us
  Pallas kernels  92.9 us (98%)
    pallas_call x1, Pallas kernels, body(): pl.pallas_call(kernel, out_shape=(jax.ShapeDtypeStruct((rows, cols), F32)...  90 us
    pallas_call x1, Pallas kernels, body(): pl.pallas_call(hand_over, out_shape=tuple((jax.ShapeDtypeStruct(r.shape,...  2.93 us

profile of v5, /device:TPU:68, one launch (start us, length us, event | category | flops | bytes accessed | tf_op | source)
XLA Modules:
  0.0 93.5 jit_solution(1719219501345052245)
XLA Ops:
  0.6 90.0 %shard_map.57 = (f32[512,256]{1,0:T(8,128)}, bf16[64,3072]{1,0:T(8,128)(2,1)}, f32[64,256]{1,0:T(8,128)}, bf16[3072,256]{1,0:T(8,128)(2,1)}) custom-call(bf16[3072,256]{1,0:T(8,128)(2,1)} %snaps.1, bf16[64,4096]{1,0:T(8,128)(2,1)} %bitcast.3), custom_call_target="tpu_custom_call" | custom-call | tf_op jit(solution)/shard_map/pallas_call | solution.py:414
  90.6 2.9 %shard_map.58 = (f32[512,256]{1,0:T(8,128)}, bf16[64,3072]{1,0:T(8,128)(2,1)}, f32[64,256]{1,0:T(8,128)}, bf16[3072,256]{1,0:T(8,128)(2,1)}) custom-call(f32[512,256]{1,0:T(8,128)} %get-tuple-element.12.refs_0_, bf16[64,3072]{1,0:T(8,128)(2,1)} %get-tuple-element.13.refs_1_, f32[64,256]{1,0:T(8,128)} %get-tuple-element.14.refs_2_, ...), custom_call_target="tpu_custom_call" | custom-call | tf_op jit(solution)/shard_map/pallas_call | solution.py:476

commit v6 on v5

--- a/solution.py
+++ b/solution.py
@@ -324,12 +324,13 @@
 
     late_two(1, 1)
     late_two(2, 1)
+    pass_on(yl == 0)
+    deliver(yl == 1)
     for k in range(3):
         wait_for(weights.at[k], w_recv.at[k])
     weight_sum[...] = (weight[...] + weights[0]) + (weights[1] + weights[2])
     copy(weight_sum, weights.at[3], w_send.at[3], w_recv.at[3], beside)
-    pass_on(yl == 0)
-    deliver(yl == 1)
+    pass_on(yl == 1)
     wait_for(weights.at[3], w_recv.at[3])
     both = weight_sum[...] + weights[3]
     scale = lax.rsqrt(both[:, cols : cols + 1] / total_cells)
@@ -350,7 +351,6 @@
         slow = slow + lax.dot_general(block, low, (((0,), (0,)), ((), ())), preferred_element_type=F32)
         resid[at, :] = (own[at, :].astype(F32) - slow / root).astype(BF16)
 
-    pass_on(yl == 1)
 
     @pl.when(role == 0)
     def _():

time: 95.2 us -> 92.1 us (0.967)
  Pallas kernels: 92.9 us -> 90.6 us
    pallas_call x1, Pallas kernels: 90 us -> 87.7 us  [body(): pl.pallas_call(kernel, out_shape=(jax.ShapeDtypeStruct((rows, cols), F32)...]
where the time goes in v6:
time: 92.1 us; the launch traced here: 91.2 us
  Pallas kernels  90.6 us (98%)
    pallas_call x1, Pallas kernels, body(): pl.pallas_call(kernel, out_shape=(jax.ShapeDtypeStruct((rows, cols), F32)...  87.7 us
    pallas_call x1, Pallas kernels, body(): pl.pallas_call(hand_over, out_shape=tuple((jax.ShapeDtypeStruct(r.shape,...  2.93 us

profile of v6, /device:TPU:68, one launch (start us, length us, event | category | flops | bytes accessed | tf_op | source)
XLA Modules:
  0.0 91.2 jit_solution(3161583056909402621)
XLA Ops:
  0.6 87.7 %shard_map.57 = (f32[512,256]{1,0:T(8,128)}, bf16[64,3072]{1,0:T(8,128)(2,1)}, f32[64,256]{1,0:T(8,128)}, bf16[3072,256]{1,0:T(8,128)(2,1)}) custom-call(bf16[3072,256]{1,0:T(8,128)(2,1)} %snaps.1, bf16[64,4096]{1,0:T(8,128)(2,1)} %bitcast.3), custom_call_target="tpu_custom_call" | custom-call | tf_op jit(solution)/shard_map/pallas_call | solution.py:414
  88.3 2.9 %shard_map.58 = (f32[512,256]{1,0:T(8,128)}, bf16[64,3072]{1,0:T(8,128)(2,1)}, f32[64,256]{1,0:T(8,128)}, bf16[3072,256]{1,0:T(8,128)(2,1)}) custom-call(f32[512,256]{1,0:T(8,128)} %get-tuple-element.12.refs_0_, bf16[64,3072]{1,0:T(8,128)(2,1)} %get-tuple-element.13.refs_1_, f32[64,256]{1,0:T(8,128)} %get-tuple-element.14.refs_2_, ...), custom_call_target="tpu_custom_call" | custom-call | tf_op jit(solution)/shard_map/pallas_call | solution.py:476

commit v7 on v6

--- a/solution.py
+++ b/solution.py
@@ -394,8 +394,17 @@
 
 def hand_over(*refs):
     sources, targets, held, sems = refs[:4], refs[4:8], refs[8:12], refs[12]
-    inward = [pltpu.make_async_copy(sources[k], held[k], sems.at[0, k]) for k in range(4)]
-    outward = [pltpu.make_async_copy(held[k], targets[k], sems.at[1, k]) for k in range(4)]
+    parts = [(k, i) for i in range(4) for k in (3, 0, 1, 2)]
+
+    def part_of(ref, i):
+        rows = ref.shape[0] // 4
+        return ref.at[pl.ds(i * rows, rows)]
+
+    inward, outward = [], []
+    for k, i in parts:
+        slot = part_of(held[k], i)
+        inward.append(pltpu.make_async_copy(part_of(sources[k], i), slot, sems.at[0, k, i]))
+        outward.append(pltpu.make_async_copy(slot, part_of(targets[k], i), sems.at[1, k, i]))
     for one in inward:
         one.start()
     for first, then in zip(inward, outward):
@@ -478,7 +487,7 @@
         out_shape=tuple(jax.ShapeDtypeStruct(r.shape, r.dtype) for r in results),
         in_specs=[pl.BlockSpec(memory_space=pl.ANY)] * 4,
         out_specs=[pl.BlockSpec(memory_space=pl.ANY)] * 4,
-        scratch_shapes=[*(pltpu.VMEM(r.shape, r.dtype) for r in results), dma((2, 4))],
+        scratch_shapes=[*(pltpu.VMEM(r.shape, r.dtype) for r in results), dma((2, 4, 4))],
     )(*results)
     return gram, modes.T, amps.T, resid
 

time: 92.1 us -> 91.9 us (level)
  no operation moved by 1% of the time
where the time goes in v7:
time: 91.9 us; the launch traced here: 91 us
  Pallas kernels  90.4 us (98%)
    pallas_call x1, Pallas kernels, body(): pl.pallas_call(kernel, out_shape=(jax.ShapeDtypeStruct((rows, cols), F32)...  87.7 us
    pallas_call x1, Pallas kernels, body(): pl.pallas_call(hand_over, out_shape=tuple((jax.ShapeDtypeStruct(r.shape,...  2.74 us

profile of v7, /device:TPU:68, one launch (start us, length us, event | category | flops | bytes accessed | tf_op | source)
XLA Modules:
  0.0 91.0 jit_solution(15736513446442198528)
XLA Ops:
  0.6 87.7 %shard_map.57 = (f32[512,256]{1,0:T(8,128)}, bf16[64,3072]{1,0:T(8,128)(2,1)}, f32[64,256]{1,0:T(8,128)}, bf16[3072,256]{1,0:T(8,128)(2,1)}) custom-call(bf16[3072,256]{1,0:T(8,128)(2,1)} %snaps.1, bf16[64,4096]{1,0:T(8,128)(2,1)} %bitcast.3), custom_call_target="tpu_custom_call" | custom-call | tf_op jit(solution)/shard_map/pallas_call | solution.py:423
  88.3 2.7 %shard_map.58 = (f32[512,256]{1,0:T(8,128)}, bf16[64,3072]{1,0:T(8,128)(2,1)}, f32[64,256]{1,0:T(8,128)}, bf16[3072,256]{1,0:T(8,128)(2,1)}) custom-call(f32[512,256]{1,0:T(8,128)} %get-tuple-element.12.refs_0_, bf16[64,3072]{1,0:T(8,128)(2,1)} %get-tuple-element.13.refs_1_, f32[64,256]{1,0:T(8,128)} %get-tuple-element.14.refs_2_, ...), custom_call_target="tpu_custom_call" | custom-call | tf_op jit(solution)/shard_map/pallas_call | solution.py:485
